TPU v7x, 512 devices: a whole 4x4x16 slice. The times are simulated.
512 devices in a mesh: row: 32 (over z, core), col: 16 (over y, x).
Axes of the slice: x: 4, y: 4, z: 16, core: 2. Of those that a mesh axis runs over, the one named last changes fastest.
Arguments:
- queries: bfloat16 [32, 1024, 256], P('row', 'col'), may hold values from -32 to 32
- key_lanes: bfloat16 [16, 2048, 256], P('col'), may hold values from -6 to 6
- values: bfloat16 [16, 2048, 256], P('col'), may hold values from -6 to 6
- grad_out: bfloat16 [32, 1024, 256], P('row', 'col'), may hold values from -6 to 6
- pattern: int32 [32, 16, 28], P('row', 'col'), may hold values from 0 to 127, as said below
- counts: int32 [32, 16], P('row', 'col'), may hold values from 8 to 28
Outputs:
- attended: bfloat16 [32, 1024, 256], P('row', 'col')
- grad_queries: bfloat16 [32, 1024, 256], P('row', 'col')
- grad_keys: bfloat16 [16, 2048, 256], P('col', 'row')
- grad_values: bfloat16 [16, 2048, 256], P('col', 'row')
Inputs may be any that keep to these rules, and one draw needn't show every extreme that they name: The entries of pattern[g, c] are distinct; only the first counts[g, c] of them are used, and among those every query block of the group appears.
All inputs are finite; a program needn't handle non-finite values.
Results may differ from a plain program's by a relative error of at most 0.025.
Values may be sent and summed in bfloat16 or wider, within the bound.
A program may use at most 64 MiB of HBM per device.

v0:
```python
import math

import jax
import jax.numpy as jnp
from jax import lax
from jax.sharding import PartitionSpec as P

D = 256
H = 8
HD = 32
BLK = 128


neg_fill = -1e30


def head_split(matrix):
    return matrix.reshape(matrix.shape[0], H, HD)


def block_scores(q_block, k_block):
    return jnp.einsum(
        "qhd,khd->hqk", head_split(q_block), head_split(k_block), preferred_element_type=jnp.float32
    ) / math.sqrt(HD)


def local_max(group_q, lanes_c, cell_list, pair_count, key_blocks):

    def local_add_pair(i, best_rows):
        cell = cell_list[i]
        q_start = cell // key_blocks * BLK
        k_start = cell % key_blocks * BLK
        scores = block_scores(
            lax.dynamic_slice_in_dim(group_q, q_start, BLK, 0),
            lax.dynamic_slice_in_dim(lanes_c, k_start, BLK, 0),
        )
        previous = lax.dynamic_slice_in_dim(best_rows, q_start, BLK, 0)
        return lax.dynamic_update_slice_in_dim(
            best_rows, jnp.maximum(previous, jnp.max(scores, axis=2).T), q_start, 0
        )

    start_max = jnp.full((group_q.shape[0], H), neg_fill, jnp.float32)
    return lax.fori_loop(jnp.int32(0), pair_count, local_add_pair, start_max)


def forward_sums(group_q, lanes_c, values_c, cell_list, pair_count, key_blocks, row_max):
    rows = group_q.shape[0]

    def forward_add_pair(i, carry):
        totals, weighted = carry
        cell = cell_list[i]
        q_start = cell // key_blocks * BLK
        k_start = cell % key_blocks * BLK
        scores = block_scores(
            lax.dynamic_slice_in_dim(group_q, q_start, BLK, 0),
            lax.dynamic_slice_in_dim(lanes_c, k_start, BLK, 0),
        )
        top = lax.dynamic_slice_in_dim(row_max, q_start, BLK, 0)
        probs = jnp.exp(scores - top.T[:, :, None])
        probs_bf = probs.astype(jnp.bfloat16)
        v_block = head_split(lax.dynamic_slice_in_dim(values_c, k_start, BLK, 0))
        mixed = jnp.einsum(
            "hqk,khd->qhd", probs_bf, v_block, preferred_element_type=jnp.float32
        ).reshape(BLK, D)
        old_tot = lax.dynamic_slice_in_dim(totals, q_start, BLK, 0)
        old_wei = lax.dynamic_slice_in_dim(weighted, q_start, BLK, 0)
        totals = lax.dynamic_update_slice_in_dim(
            totals, old_tot + jnp.sum(probs, axis=2).T, q_start, 0
        )
        weighted = lax.dynamic_update_slice_in_dim(weighted, old_wei + mixed, q_start, 0)
        return (totals, weighted)

    start = (jnp.zeros((rows, H), jnp.float32), jnp.zeros((rows, D), jnp.float32))
    return lax.fori_loop(jnp.int32(0), pair_count, forward_add_pair, start)


def add_rows(total, start_row, addend):
    return lax.dynamic_update_slice_in_dim(
        total, lax.dynamic_slice_in_dim(total, start_row, BLK, 0) + addend, start_row, 0
    )


def backward(
    group_q, group_g, lanes_c, values_c, cell_list, pair_count, key_blocks, log_total, row_dots
):
    scale = 1.0 / math.sqrt(HD)
    rows = group_q.shape[0]
    lanes = lanes_c.shape[0]

    def backward_add_pair(i, carry):
        cell = cell_list[i]
        q_start = cell // key_blocks * BLK
        k_start = cell % key_blocks * BLK
        q_block = lax.dynamic_slice_in_dim(group_q, q_start, BLK, 0)
        k_block = lax.dynamic_slice_in_dim(lanes_c, k_start, BLK, 0)
        v_block = lax.dynamic_slice_in_dim(values_c, k_start, BLK, 0)
        g_block = lax.dynamic_slice_in_dim(group_g, q_start, BLK, 0)
        scores = block_scores(q_block, k_block)
        norm_rows = lax.dynamic_slice_in_dim(log_total, q_start, BLK, 0)
        dot_rows = lax.dynamic_slice_in_dim(row_dots, q_start, BLK, 0)
        weights = jnp.exp(scores - norm_rows.T[:, :, None])
        g_heads = head_split(g_block)
        dprob = jnp.einsum(
            "qhd,khd->hqk", g_heads, head_split(v_block), preferred_element_type=jnp.float32
        )
        dscore = weights * (dprob - dot_rows.T[:, :, None])
        dscore_bf = dscore.astype(jnp.bfloat16)
        updated = []
        place = 0
        new_q = (
            jnp.einsum(
                "hqk,khd->qhd", dscore_bf, head_split(k_block), preferred_element_type=jnp.float32
            ).reshape(BLK, D)
            * scale
        )
        updated.append(add_rows(carry[place], q_start, new_q))
        place = place + 1
        weights_bf = weights.astype(jnp.bfloat16)
        new_v = jnp.einsum(
            "hqk,qhd->khd", weights_bf, g_heads, preferred_element_type=jnp.float32
        ).reshape(BLK, D)
        new_k = (
            jnp.einsum(
                "hqk,qhd->khd", dscore_bf, head_split(q_block), preferred_element_type=jnp.float32
            ).reshape(BLK, D)
            * scale
        )
        updated.append(add_rows(carry[place], k_start, new_k))
        updated.append(add_rows(carry[place + 1], k_start, new_v))
        return tuple(updated)

    start = []
    start.append(jnp.zeros((rows, D), jnp.float32))
    start.append(jnp.zeros((lanes, D), jnp.float32))
    start.append(jnp.zeros((lanes, D), jnp.float32))
    return lax.fori_loop(jnp.int32(0), pair_count, backward_add_pair, tuple(start))


def reduce_keys(grad_k, grad_v):
    return (
        lax.psum_scatter(
            grad_k.astype(jnp.bfloat16), "row", scatter_dimension=0, tiled=True
        ).astype(jnp.float32),
        lax.psum_scatter(
            grad_v.astype(jnp.bfloat16), "row", scatter_dimension=0, tiled=True
        ).astype(jnp.float32),
    )


def shards(queries, key_lanes, values, grad_out, pattern, counts):
    own_q = queries[0]
    own_g = grad_out[0]
    own_rows = own_q.shape[0]
    group_q, group_g = (
        lax.all_gather(own_q, "col", axis=0, tiled=True),
        lax.all_gather(own_g, "col", axis=0, tiled=True),
    )
    lanes_c = key_lanes[0]
    values_c = values[0]
    cell_list = pattern[0, 0]
    pair_count = counts[0, 0]
    key_blocks = lanes_c.shape[0] // BLK
    group_rows = group_q.shape[0]
    row_start = lax.axis_index("col") * own_rows
    local_top = local_max(group_q, lanes_c, cell_list, pair_count, key_blocks)
    row_max = lax.pmax(local_top, "col")
    totals, weighted = forward_sums(
        group_q, lanes_c, values_c, cell_list, pair_count, key_blocks, row_max
    )
    totals, weighted = lax.psum((totals, weighted), "col")
    log_total = row_max + jnp.log(totals)
    normed = (head_split(weighted) / totals[:, :, None]).reshape(group_rows, D)
    row_dots = jnp.sum(head_split(group_g).astype(jnp.float32) * head_split(normed), axis=2)
    attended = lax.dynamic_slice_in_dim(normed, row_start, own_rows, 0).astype(jnp.bfloat16)
    grad_q, grad_k, grad_v = backward(
        group_q, group_g, lanes_c, values_c, cell_list, pair_count, key_blocks, log_total, row_dots
    )
    own_grad_k, own_grad_v = reduce_keys(grad_k, grad_v)
    own_grad_q = lax.psum_scatter(grad_q, "col", scatter_dimension=0, tiled=True)
    return (
        attended[None],
        own_grad_q.astype(jnp.bfloat16)[None],
        own_grad_k.astype(jnp.bfloat16)[None],
        own_grad_v.astype(jnp.bfloat16)[None],
    )


def solution(mesh):
    return jax.shard_map(
        shards,
        mesh=mesh,
        in_specs=(
            P("row", "col", None),
            P("col", None, None),
            P("col", None, None),
            P("row", "col", None),
            P("row", "col", None),
            P("row", "col"),
        ),
        out_specs=(
            P("row", "col", None),
            P("row", "col", None),
            P("col", "row", None),
            P("col", "row", None),
        ),
        check_vma=False,
    )
```

profile of v0, /device:TPU:1, one launch (start us, length us, event | category | flops | bytes accessed | tf_op | source)
XLA Modules:
  0.0 1151.1 jit_solution(11253190356890599533)
XLA Ops:
  7.2 20.1 %all-gather = bf16[1,1024,256]{2,1,0:T(8,128)(2,1)S(1)} all-gather(bf16[1,64,256]{2,1,0:T(8,128)(2,1)} %param.12), channel_id=2, replica_groups=mesh['row'=32,'col'=16] {'col'}, dimensions={1}, use_global_device_ids=true | all-gather | bytes 557056 | tf_op jit(solution)/shard_map/all_gather | solution.py:155
  28.2 38.8 %while.42 = (s32[]{:T(128)}, f32[1024,8]{0,1:T(8,128)S(1)}, s32[]{:T(128)}, s32[28]{0:T(128)S(1)}, bf16[1024,256]{0,1:T(8,128)(2,1)S(1)}, /*index=5*/bf16[2048,2...) while((s32[]{:T(128)}, f32[1024,8]{0,1:T(8,128)S(1)}, ...), condition=%wide.region_2.3_spmd, body=%wide.region_0.2_spmd.sunk | while | flops 8650784 | bytes 410094 | solution.py:43
  67.0 58.0 %pmax.7 = f32[1024,8]{0,1:T(8,128)S(1)} all-reduce(f32[1024,8]{0,1:T(8,128)S(1)} %get-tuple-element.364), channel_id=1, replica_groups=mesh['row'=32,'col'=16] {'col'}, use_global_device_ids=true, to_apply=%region_3.4 | all-reduce | flops 8192 | bytes 65536 | tf_op jit(solution)/shard_map/pmax | solution.py:166
  125.0 2.3 copy.33
  127.4 49.3 %while.43 = (s32[]{:T(128)}, f32[1024,8]{0,1:T(8,128)S(1)}, f32[1024,256]{0,1:T(8,128)S(1)}, s32[]{:T(128)}, s32[28]{0:T(128)S(1)}, /*index=5*/bf16[1024,256]{0,...) while((s32[]{:T(128)}, f32[1024,8]{0,1:T(8,128)S(1)}, ...), condition=%wide.region_6.7_spmd, body=%wide.region_4.6_spmd.sunk | while | flops 17334304 | bytes 1667598 | solution.py:74
  176.7 1.0 copy-done
  177.7 18.2 %all-gather.1 = bf16[1,1024,256]{2,1,0:T(8,128)(2,1)} all-gather(bf16[1,64,256]{2,1,0:T(8,128)(2,1)S(1)} %copy-done.11), channel_id=3, replica_groups=mesh['row'=32,'col'=16] {'col'}, dimensions={1}, use_global_device_ids=true | all-gather | bytes 557056 | tf_op jit(solution)/shard_map/all_gather | solution.py:156
  195.9 1.1 bitcast_convert_fusion
  197.4 57.9 %psum.15 = f32[1024,8]{0,1:T(8,128)S(1)} all-reduce(f32[1024,8]{0,1:T(8,128)S(1)} %get-tuple-element.366), channel_id=1, replica_groups=mesh['row'=32,'col'=16] {'col'}, use_global_device_ids=true, to_apply=%region_8.9 | all-reduce | flops 8192 | bytes 65536 | tf_op jit(solution)/shard_map/psum | solution.py:170
  255.3 239.7 %all-reduce.2.cloned.1.call-done = f32[1024,256]{0,1:T(8,128)} async-done(((f32[1024,256]{0,1:T(8,128)}), f32[1024,256]{0,1:T(8,128)}) %all-reduce.2.cloned.1.call-update) | async-done | bytes 1048592 | tf_op jit(solution)/shard_map/psum | solution.py:170
  495.0 1.5 multiply_reduce_fusion
  496.5 1.1 broadcast.51.clone
  497.7 1.5 broadcast.52.clone
  499.2 109.8 %while.44 = (s32[]{:T(128)}, f32[1024,256]{1,0:T(8,128)}, f32[2048,256]{1,0:T(8,128)}, f32[2048,256]{1,0:T(8,128)S(1)}, s32[]{:T(128)}, /*index=5*/s32[28]{0:T(1...) while((s32[]{:T(128)}, f32[1024,256]{1,0:T(8,128)}, ...), condition=%wide.region_11.12_spmd, body=%wide.region_10.11_spmd.sunk | while | flops 42893344 | bytes 12935906 | solution.py:136
  507.1 0.9 constant_dynamic-slice_fusion.27
  519.2 0.9 constant_dynamic-slice_fusion.27
  531.4 0.9 constant_dynamic-slice_fusion.27
  541.6 0.9 constant_dynamic-slice_fusion.23
  543.5 0.9 constant_dynamic-slice_fusion.27
  553.7 0.9 constant_dynamic-slice_fusion.23
  555.6 0.9 constant_dynamic-slice_fusion.27
  567.7 0.9 constant_dynamic-slice_fusion.27
  579.9 0.9 constant_dynamic-slice_fusion.27
  592.0 0.9 constant_dynamic-slice_fusion.27
  604.1 0.9 constant_dynamic-slice_fusion.27
  609.1 1.1 convert_element_type.45
  610.3 2.7 convert_element_type.44
  613.1 1.0 fusion.14
  614.9 310.6 %reduce-scatter.4.cloned.1.call-done = f32[64,256]{1,0:T(8,128)} async-done(((f32[1024,256]{1,0:T(8,128)}), f32[64,256]{1,0:T(8,128)}) %reduce-scatter.4.cloned.1.call-update) | async-done | bytes 65552 | tf_op jit(solution)/shard_map/reduce_scatter | solution.py:179
  925.5 1.5 convert_bitcast_fusion
  926.9 108.5 %reduce-scatter.8.cloned.1.call-done = bf16[64,256]{1,0:T(8,128)(2,1)} async-done(((bf16[2048,256]{1,0:T(8,128)(2,1)}), bf16[64,256]{1,0:T(8,128)(2,1)}) %reduce-scatter.8.cloned.1.call-update) | async-done | bytes 32784 | tf_op jit(solution)/shard_map/reduce_scatter | solution.py:144
  1035.4 109.2 %reduce-scatter.6.cloned.1.call-done = bf16[64,256]{1,0:T(8,128)(2,1)} async-done(((bf16[2048,256]{1,0:T(8,128)(2,1)}), bf16[64,256]{1,0:T(8,128)(2,1)}) %reduce-scatter.6.cloned.1.call-update) | async-done | bytes 32784 | tf_op jit(solution)/shard_map/reduce_scatter | solution.py:141
  (461 shorter events, 96.0 us)
Async XLA Ops:
  7.2 20.4 %copy-start.4 = (bf16[1,2048,256]{2,1,0:T(8,128)(2,1)S(1)}, bf16[1,2048,256]{2,1,0:T(8,128)(2,1)}, u32[]{:S(2)}) copy-start(bf16[1,2048,256]{2,1,0:T(8,128)(2,1)} %param.13) | copy-start | bytes 3145732
  7.2 21.1 %copy-start.12 = (s32[1,1,28]{2,1,0:T(1,128)S(1)}, s32[1,1,28]{2,1,0:T(1,128)}, u32[]{:S(2)}) copy-start(s32[1,1,28]{2,1,0:T(1,128)} %param.16) | copy-start | bytes 340
  7.2 487.8 %all-reduce.2.cloned.1.call-start = ((), (), s32[]{:S(2)}) async-start(), calls=%async_computation.3 | async-start | bytes 2097152 | tf_op jit(solution)/shard_map/psum | solution.py:170
  67.0 60.3 %copy-start.3 = (bf16[2048,256]{0,1:T(8,128)(2,1)}, bf16[2048,256]{0,1:T(8,128)(2,1)S(1)}, u32[]{:S(2)}) copy-start(bf16[2048,256]{0,1:T(8,128)(2,1)S(1)} %get-tuple-element.848) | copy-start | bytes 3145732
  127.4 50.3 %copy-start.11 = (bf16[1,64,256]{2,1,0:T(8,128)(2,1)S(1)}, bf16[1,64,256]{2,1,0:T(8,128)(2,1)}, u32[]{:S(2)}) copy-start(bf16[1,64,256]{2,1,0:T(8,128)(2,1)} %param.15) | copy-start | bytes 98308
  177.7 747.8 %reduce-scatter.4.cloned.1.call-start = ((), (), s32[]{:S(2)}) async-start(), calls=%async_computation.4 | async-start | bytes 1114112 | tf_op jit(solution)/shard_map/reduce_scatter | solution.py:179
  255.3 241.2 %copy-start.5 = (f32[1024,8]{0,1:T(8,128)}, f32[1024,8]{0,1:T(8,128)S(1)}, u32[]{:S(2)}) copy-start(f32[1024,8]{0,1:T(8,128)S(1)} %psum.15) | copy-start | bytes 98308
  499.8 8.7 copy-start.7
  499.9 8.9 copy-start.1
  512.0 8.7 copy-start.7
  512.0 8.7 copy-start.9
  512.0 8.9 copy-start.1
  524.1 8.7 copy-start.7
  524.1 8.7 copy-start.9
  524.1 8.9 copy-start.1
  536.2 8.7 copy-start.7
  536.3 8.7 copy-start.9
  536.3 8.9 copy-start.1
  548.4 8.7 copy-start.7
  548.4 8.7 copy-start.9
  548.4 8.9 copy-start.1
  560.5 8.7 copy-start.7
  560.5 8.9 copy-start.1
  572.6 8.7 copy-start.7
  572.6 8.7 copy-start.9
  572.6 8.9 copy-start.1
  584.7 8.7 copy-start.7
  584.8 8.9 copy-start.1
  596.9 8.7 copy-start.7
  596.9 8.9 copy-start.1
  609.0 426.4 %reduce-scatter.8.cloned.1.call-start = ((), (), s32[]{:S(2)}) async-start(), calls=%async_computation.6 | async-start | bytes 1081344 | tf_op jit(solution)/shard_map/reduce_scatter | solution.py:144
  610.2 534.4 %reduce-scatter.6.cloned.1.call-start = ((), (), s32[]{:S(2)}) async-start(), calls=%async_computation.5 | async-start | bytes 1081344 | tf_op jit(solution)/shard_map/reduce_scatter | solution.py:141
  (33 other events, 86.5 us)
Sparse Core Ops, SparseCore 0:
  177.8 317.1 all-reduce.1
  609.2 316.2 reduce-scatter.3
  929.1 106.3 reduce-scatter.7
  1038.6 105.9 reduce-scatter.5
where the time goes:
time: 1160 us; the launch traced here: 1150 us
  waiting for transfers between devices  768 us (66%)
  blocking collectives  154 us (13%)
  loops' own time  94.2 us (8%)
  local copies, waits for them, and re-layouts  92.1 us (8%)
  matrix products  18.5 us (2%)
  between operations  14 us (1%)
    reduce_scatter x1, waiting for transfers between devices, shards(): lax.psum_scatter(grad_q, 'col', scatter_dimension=0, tiled=True)  311 us
    psum x1, waiting for transfers between devices, shards(): totals, weighted = lax.psum((totals, weighted), 'col')  240 us
    reduce_scatter x1, waiting for transfers between devices, reduce_keys(): lax.psum_scatter(grad_k.astype(jnp.bfloat16), 'row', scatter_dimension=0,...  109 us
    reduce_scatter x1, waiting for transfers between devices, reduce_keys(): lax.psum_scatter(grad_v.astype(jnp.bfloat16), 'row', scatter_dimension=0,...  109 us
    pmax x1, blocking collectives, shards(): row_max = lax.pmax(local_top, 'col')  58 us
    psum x1, blocking collectives, shards(): totals, weighted = lax.psum((totals, weighted), 'col')  57.9 us
    another operation x1, loops' own time, backward(): lax.fori_loop(jnp.int32(0), pair_count, backward_add_pair, tuple(start))  33.1 us
    another operation x1, loops' own time, forward_sums(): return lax.fori_loop(jnp.int32(0), pair_count, forward_add_pair, start)  30.7 us
  transfers between devices with their start and end apart: 4, of which 4 were waited for; matrix products, arithmetic and copies ran while one was open for 1% of the time, Pallas kernels for 0%

commit v1 on v0

v1 whole, which is shorter than its diff:
```python
import functools
import math

import jax
import jax.numpy as jnp
from jax import lax
from jax.experimental import pallas as pl
from jax.experimental.pallas import tpu as pltpu
from jax.sharding import PartitionSpec as P

D = 256
H = 8
HD = 32
BLK = 128
HALF = D // 2
HH = H // 2
MESH = pl.DeviceIdType.MESH
SCALE = 1.0 / math.sqrt(HD)
LOG2E = math.log2(math.e)
SCALE2 = SCALE * LOG2E
NEG = -1e30
VMEM_LIMIT = 56 * 1024 * 1024

vmem = pl.BlockSpec(memory_space=pltpu.VMEM)
smem = pl.BlockSpec(memory_space=pltpu.SMEM)


def call(kernel, name, out_shape, n_smem, n_vmem, scratch, collective_id=None):
    return pl.pallas_call(
        kernel,
        name=name,
        out_shape=out_shape,
        in_specs=[smem] * n_smem + [vmem] * n_vmem,
        out_specs=jax.tree.map(lambda _: vmem, out_shape),
        scratch_shapes=scratch,
        compiler_params=pltpu.CompilerParams(
            collective_id=collective_id,
            has_side_effects=collective_id is not None,
            vmem_limit_bytes=VMEM_LIMIT,
        ),
    )


def meet(peers):
    barrier = pltpu.get_barrier_semaphore()
    for peer in peers:
        pl.semaphore_signal(barrier, inc=1, device_id=peer, device_id_type=MESH)
    pl.semaphore_wait(barrier, len(peers))


def remote(src, dst, send_sem, recv_sem, device):
    return pltpu.make_async_remote_copy(
        src_ref=src,
        dst_ref=dst,
        send_sem=send_sem,
        recv_sem=recv_sem,
        device_id=device,
        device_id_type=MESH,
    )


def others(me, n):
    return [lax.rem(me + k, n) for k in range(1, n)]


def senders(me, n):
    return [lax.rem(me + n - k, n) for k in range(1, n)]


def head_mask(h):
    lane = lax.broadcasted_iota(jnp.int32, (BLK, D), 1)
    return jnp.where((lane >= h * HD) & (lane < (h + 1) * HD), 1.0, 0.0).astype(jnp.bfloat16)


def block_diagonal(refs, outs):
    blocks = outs[0].shape[0]
    for h in range(H):
        mask = head_mask(h)

        def one(b, carry):
            rows = pl.ds(pl.multiple_of(b * BLK, BLK), BLK)
            for ref, out in zip(refs, outs):
                out[b, h * BLK : (h + 1) * BLK, :] = ref[rows, :] * mask
            return carry

        lax.fori_loop(0, blocks, one, 0)


def dot_nt(a, b):
    return lax.dot_general(a, b, (((1,), (1,)), ((), ())), preferred_element_type=jnp.float32)


def dot(a, b):
    return jnp.dot(a, b, preferred_element_type=jnp.float32)


def gather_kernel(n, q_ref, g_ref, k_ref, v_ref, qo, go, kt, vt, send_sem, recv_sem):
    row, me = lax.axis_index("row"), lax.axis_index("col")
    peers = others(me, n)
    meet([(row, p) for p in peers])
    sends = []
    for i, (src, dst) in enumerate(((q_ref, qo), (g_ref, go))):
        for p in peers:
            copy = remote(src, dst.at[me], send_sem.at[i, p], recv_sem.at[i, me], (row, p))
            copy.start()
            sends.append(copy)
    qo[me] = q_ref[...]
    go[me] = g_ref[...]

    def turn(b, carry):
        rows = pl.ds(pl.multiple_of(b * BLK, BLK), BLK)
        kt[:, rows] = k_ref[rows, :].T
        vt[:, rows] = v_ref[rows, :].T
        return carry

    lax.fori_loop(0, k_ref.shape[0] // BLK, turn, 0)
    for i, (src, dst) in enumerate(((q_ref, qo), (g_ref, go))):
        for p in senders(me, n):
            remote(src, dst.at[p], send_sem.at[i, p], recv_sem.at[i, p], (row, p)).wait_recv()
    for copy in sends:
        copy.wait_send()


def forward_kernel(key_blocks, cells, count, q_ref, k_ref, vt_ref, part, stat, qbd, acc, top, tot):
    block_diagonal((q_ref,), (qbd,))
    acc[...] = jnp.zeros_like(acc)
    tot[...] = jnp.zeros_like(tot)
    top[...] = jnp.full_like(top, NEG)

    def pair(j, carry):
        cell = cells[0, j]
        qb = cell // key_blocks
        q_at = pl.ds(pl.multiple_of(qb * BLK, BLK), BLK)
        k_at = pl.ds(pl.multiple_of(cell % key_blocks * BLK, BLK), BLK)
        scores = dot_nt(k_ref[k_at, :], qbd[qb])
        old = top[:, q_at]
        best = [
            jnp.max(scores[:, h * BLK : (h + 1) * BLK], axis=0, keepdims=True) for h in range(H)
        ]
        new = jnp.maximum(old, jnp.concatenate(best, axis=0) * SCALE2)
        fade = jnp.exp2(old - new)
        top[:, q_at] = new
        sums = []
        for h in range(H):
            probs = jnp.exp2(scores[:, h * BLK : (h + 1) * BLK] * SCALE2 - new[h : h + 1])
            sums.append(jnp.sum(probs, axis=0, keepdims=True))
            at = slice(h * HD, (h + 1) * HD)
            mixed = dot(vt_ref[at, k_at], probs.astype(jnp.bfloat16))
            acc[at, q_at] = acc[at, q_at] * fade[h : h + 1] + mixed
        tot[:, q_at] = tot[:, q_at] * fade + jnp.concatenate(sums, axis=0)
        return carry

    lax.fori_loop(0, count[0, 0], pair, 0)
    for b in range(qbd.shape[0]):
        lanes = slice(b * BLK, (b + 1) * BLK)
        for half in range(2):
            part[2 * b + half] = acc[half * HALF : (half + 1) * HALF, lanes].astype(jnp.bfloat16)
            heads = slice(half * HH, (half + 1) * HH)
            stat[2 * b + half] = jnp.concatenate([top[heads, lanes], tot[heads, lanes]], axis=0)


def swap_halves(own, out, got, mine, send_sem, recv_sem, row, me):
    half = lax.rem(me, 2)
    rows = BLK // 2
    own_at = pl.ds(pl.multiple_of(half * rows, rows), rows)
    other_at = pl.ds(pl.multiple_of((1 - half) * rows, rows), rows)
    mine[...] = own
    copy = remote(mine.at[other_at], got, send_sem, recv_sem, (row, me + 1 - 2 * half))
    copy.start()

    def finish():
        out[:, pl.ds(pl.multiple_of(half * HALF, HALF), HALF)] = mine[own_at, :]
        copy.wait_recv()
        out[:, pl.ds(pl.multiple_of((1 - half) * HALF, HALF), HALF)] = got[...]
        copy.wait_send()

    return finish


def combine_kernel(
    n, part, stat, g_ref, att, logs, parts, stats, mine, got, part_sems, stat_sems, log_sems, swap_sems
):
    row, me = lax.axis_index("row"), lax.axis_index("col")
    peers, sources = others(me, n), senders(me, n)
    meet([(row, p) for p in peers])
    sends = []
    for src, dst, sems in ((stat, stats, stat_sems), (part, parts, part_sems)):
        for p in peers:
            copy = remote(src.at[p], dst.at[me], sems.at[0, p], sems.at[1, me], (row, p))
            copy.start()
            sends.append(copy)
    block, half = me // 2, lax.rem(me, 2)
    grad = g_ref[
        pl.ds(pl.multiple_of(block * BLK, BLK), BLK), pl.ds(pl.multiple_of(half * HALF, HALF), HALF)
    ]
    grad = grad.astype(jnp.float32).T.reshape(HH, HD, BLK)
    stats[me] = stat[me]
    for p in sources:
        remote(stat.at[p], stats.at[p], stat_sems.at[0, p], stat_sems.at[1, p], (row, p)).wait_recv()
    every = stats[...]
    top = jnp.max(every[:, :HH], axis=0)
    tot = jnp.sum(every[:, HH:] * jnp.exp2(every[:, :HH] - top[None]), axis=0)

    def share(source, ref):
        fade = jnp.exp2(stats[source][:HH] - top)
        return ref[source].astype(jnp.float32).reshape(HH, HD, BLK) * fade[:, None, :]

    weighted = share(me, part)
    for p in sources:
        remote(part.at[p], parts.at[p], part_sems.at[0, p], part_sems.at[1, p], (row, p)).wait_recv()
        weighted = weighted + share(p, parts)
    normed = weighted / tot[:, None, :]
    dots = jnp.sum(grad * normed, axis=1)
    logs[me] = jnp.concatenate([top + jnp.log(tot) * LOG2E, dots], axis=0)
    for p in peers:
        copy = remote(logs.at[me], logs.at[me], log_sems.at[0, p], log_sems.at[1, me], (row, p))
        copy.start()
        sends.append(copy)
    own = normed.reshape(HALF, BLK).T.astype(jnp.bfloat16)
    swap_halves(own, att, got, mine, swap_sems.at[0], swap_sems.at[1], row, me)()
    for p in sources:
        remote(logs.at[p], logs.at[p], log_sems.at[0, p], log_sems.at[1, p], (row, p)).wait_recv()
    for copy in sends:
        copy.wait_send()


def backward_kernel(
    key_blocks, cells, count, q_ref, g_ref, k_ref, v_ref, kt_ref, logs, dq, dk, dv, qbd, gbd, dq_acc, dk_acc, dv_acc
):
    block_diagonal((q_ref, g_ref), (qbd, gbd))
    dq_acc[...] = jnp.zeros_like(dq_acc)
    dk_acc[...] = jnp.zeros_like(dk_acc)
    dv_acc[...] = jnp.zeros_like(dv_acc)

    def pair(j, carry):
        cell = cells[0, j]
        qb = cell // key_blocks
        q_at = pl.ds(pl.multiple_of(qb * BLK, BLK), BLK)
        k_at = pl.ds(pl.multiple_of(cell % key_blocks * BLK, BLK), BLK)
        scores = dot_nt(k_ref[k_at, :], qbd[qb])
        dprob = dot_nt(v_ref[k_at, :], gbd[qb])
        low, high = logs[2 * qb], logs[2 * qb + 1]
        all_weights, all_dscore = [], []
        for h in range(H):
            lanes = slice(h * BLK, (h + 1) * BLK)
            info, r = (low, h) if h < HH else (high, h - HH)
            weights = jnp.exp2(scores[:, lanes] * SCALE2 - info[r : r + 1])
            dscore = weights * (dprob[:, lanes] - info[HH + r : HH + r + 1])
            dscore = dscore.astype(jnp.bfloat16)
            all_weights.append(weights.astype(jnp.bfloat16))
            all_dscore.append(dscore)
            at = slice(h * HD, (h + 1) * HD)
            dq_acc[at, q_at] += dot(kt_ref[at, k_at], dscore)
        dv_acc[k_at, :] += dot(jnp.concatenate(all_weights, axis=1), gbd[qb])
        dk_acc[k_at, :] += dot(jnp.concatenate(all_dscore, axis=1), qbd[qb])
        return carry

    lax.fori_loop(0, count[0, 0], pair, 0)
    for b in range(qbd.shape[0]):
        for half in range(2):
            tile = dq_acc[half * HALF : (half + 1) * HALF, b * BLK : (b + 1) * BLK]
            dq[2 * b + half] = (tile * SCALE).astype(jnp.bfloat16)

    def finish(b, carry):
        at = pl.ds(pl.multiple_of(b * BLK, BLK), BLK)
        dk[at, :] = (dk_acc[at, :] * SCALE).astype(jnp.bfloat16)
        dv[at, :] = dv_acc[at, :].astype(jnp.bfloat16)
        return carry

    lax.fori_loop(0, dk.shape[0] // BLK, finish, 0)


def reduce_kernel(
    n_col, n_z, dq, dk, dv, out_q, out_k, out_v, parts, mine, got, pair, up_out, up_in, down_out, down_in,
    part_sems, pair_sems, swap_sems, up_sems, down_sems
):
    row, me = lax.axis_index("row"), lax.axis_index("col")
    z, core = row // 2, lax.rem(row, 2)
    sibling = (row + 1 - 2 * core, me)
    above = (lax.rem(z + 1, n_z) * 2 + core, me)
    below = (lax.rem(z + n_z - 1, n_z) * 2 + core, me)
    peers, sources = others(me, n_col), senders(me, n_col)
    ring = [above, below] if n_z > 2 else [above]
    meet([sibling] + ring + [(row, p) for p in peers])
    grads = (dk, dv)
    sends = []
    for i, src in enumerate(grads):
        copy = remote(src.at[:, 1 - core], pair.at[i], pair_sems.at[0, i], pair_sems.at[1, i], sibling)
        copy.start()
        sends.append(copy)
    for p in peers:
        copy = remote(dq.at[p], parts.at[me], part_sems.at[0, p], part_sems.at[1, me], (row, p))
        copy.start()
        sends.append(copy)
    for i, src in enumerate(grads):
        sends[i].wait_recv()

    def own(i, chunk):
        return grads[i][chunk, core].astype(jnp.float32) + pair[i, chunk].astype(jnp.float32)

    n_up, n_down = n_z // 2, n_z - 1 - n_z // 2
    directions = (
        (n_up, up_out, up_in, up_sems, above, below),
        (n_down, down_out, down_in, down_sems, below, above),
    )

    def arrived(i, step, direction):
        _, out, into, sems, to, _ = direction
        remote(
            out.at[i, step], into.at[i, step], sems.at[0, i, step], sems.at[1, i, step], to
        ).wait_recv()
        return into[i, step].astype(jnp.float32)

    for step in range(n_up):
        for i in range(2):
            for d, direction in enumerate(directions):
                hops, out, into, sems, to, _ = direction
                if step >= hops:
                    continue
                away = hops - step
                chunk = lax.rem(z + (away if d == 0 else n_z - away), n_z)
                value = own(i, chunk)
                if step:
                    value = value + arrived(i, step - 1, direction)
                out[i, step] = value.astype(jnp.bfloat16)
                copy = remote(
                    out.at[i, step], into.at[i, step], sems.at[0, i, step], sems.at[1, i, step], to
                )
                copy.start()
                sends.append(copy)
        if step == n_up // 2:
            total = dq[me].astype(jnp.float32)
            for p in sources:
                remote(
                    dq.at[p], parts.at[p], part_sems.at[0, p], part_sems.at[1, p], (row, p)
                ).wait_recv()
                total = total + parts[p].astype(jnp.float32)
            finish = swap_halves(
                total.T.astype(jnp.bfloat16), out_q, got, mine, swap_sems.at[0], swap_sems.at[1], row, me
            )
    finish()
    for i, out in enumerate((out_k, out_v)):
        value = own(i, z)
        for direction in directions:
            if direction[0]:
                value = value + arrived(i, direction[0] - 1, direction)
        out[...] = value.astype(jnp.bfloat16)
    for copy in sends:
        copy.wait_send()


def shards(n_row, n_col, queries, key_lanes, values, grad_out, pattern, counts):
    bf16, f32 = jnp.bfloat16, jnp.float32
    dma = pltpu.SemaphoreType.DMA
    shape = jax.ShapeDtypeStruct
    own_q, own_g, keys, vals = queries[0], grad_out[0], key_lanes[0], values[0]
    cells, count = pattern[0], counts
    own_rows, lanes = own_q.shape[0], keys.shape[0]
    rows = own_rows * n_col
    q_blocks, key_blocks, n_z = rows // BLK, lanes // BLK, n_row // 2
    chunk = lanes // n_row

    all_q, all_g, keys_t, vals_t = call(
        functools.partial(gather_kernel, n_col),
        "gather_lanes",
        (shape((n_col, own_rows, D), bf16),) * 2 + (shape((D, lanes), bf16),) * 2,
        0,
        4,
        [dma((2, n_col)), dma((2, n_col))],
        0,
    )(own_q, own_g, keys, vals)
    all_q, all_g = all_q.reshape(rows, D), all_g.reshape(rows, D)

    part, stat = call(
        functools.partial(forward_kernel, key_blocks),
        "forward_pairs",
        (shape((n_col, HALF, BLK), bf16), shape((n_col, H, BLK), f32)),
        2,
        3,
        [
            pltpu.VMEM((q_blocks, H * BLK, D), bf16),
            pltpu.VMEM((D, rows), f32),
            pltpu.VMEM((H, rows), f32),
            pltpu.VMEM((H, rows), f32),
        ],
    )(cells, count, all_q, keys, vals_t)

    attended, logs = call(
        functools.partial(combine_kernel, n_col),
        "combine_rows",
        (shape((own_rows, D), bf16), shape((n_col, H, BLK), f32)),
        0,
        3,
        [
            pltpu.VMEM((n_col, HALF, BLK), bf16),
            pltpu.VMEM((n_col, H, BLK), f32),
            pltpu.VMEM((BLK, HALF), bf16),
            pltpu.VMEM((own_rows, HALF), bf16),
            dma((2, n_col)),
            dma((2, n_col)),
            dma((2, n_col)),
            dma((2,)),
        ],
        1,
    )(part, stat, all_g)

    dq, dk, dv = call(
        functools.partial(backward_kernel, key_blocks),
        "backward_pairs",
        (shape((n_col, HALF, BLK), bf16), shape((lanes, D), bf16), shape((lanes, D), bf16)),
        2,
        6,
        [
            pltpu.VMEM((q_blocks, H * BLK, D), bf16),
            pltpu.VMEM((q_blocks, H * BLK, D), bf16),
            pltpu.VMEM((D, rows), f32),
            pltpu.VMEM((lanes, D), f32),
            pltpu.VMEM((lanes, D), f32),
        ],
    )(cells, count, all_q, all_g, keys, vals, keys_t, logs)

    n_up = n_z // 2
    n_down = max(1, n_z - 1 - n_up)
    grad_q, grad_k, grad_v = call(
        functools.partial(reduce_kernel, n_col, n_z),
        "reduce_gradients",
        (shape((own_rows, D), bf16), shape((chunk, D), bf16), shape((chunk, D), bf16)),
        0,
        3,
        [
            pltpu.VMEM((n_col, HALF, BLK), bf16),
            pltpu.VMEM((BLK, HALF), bf16),
            pltpu.VMEM((own_rows, HALF), bf16),
            pltpu.VMEM((2, n_z, chunk, D), bf16),
            pltpu.VMEM((2, n_up, chunk, D), bf16),
            pltpu.VMEM((2, n_up, chunk, D), bf16),
            pltpu.VMEM((2, n_down, chunk, D), bf16),
            pltpu.VMEM((2, n_down, chunk, D), bf16),
            dma((2, n_col)),
            dma((2, 2)),
            dma((2,)),
            dma((2, 2, n_up)),
            dma((2, 2, n_down)),
        ],
        2,
    )(dq, dk.reshape(n_z, 2, chunk, D), dv.reshape(n_z, 2, chunk, D))
    return attended[None], grad_q[None], grad_k[None], grad_v[None]


def solution(mesh):
    return jax.shard_map(
        functools.partial(shards, mesh.shape["row"], mesh.shape["col"]),
        mesh=mesh,
        in_specs=(
            P("row", "col", None),
            P("col", None, None),
            P("col", None, None),
            P("row", "col", None),
            P("row", "col", None),
            P("row", "col"),
        ),
        out_specs=(
            P("row", "col", None),
            P("row", "col", None),
            P("col", "row", None),
            P("col", "row", None),
        ),
        check_vma=False,
    )
```

time: 1160 us -> 132 us (0.11)
  the two profiles are of different devices: /device:TPU:1 before, /device:TPU:32 now
where the time goes in v1:
time: 132 us
  Pallas kernels  128 us (97%)
  local copies, waits for them, and re-layouts  2.91 us (2%)
  between operations  1.32 us (1%)
    pallas_call x1, Pallas kernels, shards(): call(functools.partial(reduce_kernel, n_col, n_z), 'reduce_gradients', (s...  64 us
    pallas_call x1, Pallas kernels, shards(): call(functools.partial(gather_kernel, n_col), 'gather_lanes', (shape((n_c...  23.1 us
    pallas_call x1, Pallas kernels, shards(): call(functools.partial(combine_kernel, n_col), 'combine_rows', (shape((ow...  21.3 us
    pallas_call x1, Pallas kernels, shards(): call(functools.partial(backward_kernel, key_blocks), 'backward_pairs', (s...  11.8 us
    pallas_call x1, Pallas kernels, shards(): call(functools.partial(forward_kernel, key_blocks), 'forward_pairs', (sha...  7.47 us
    unnamed x12, local copies, waits for them, and re-layouts  2.91 us

profile of v1, /device:TPU:32, one launch (start us, length us, event | category | flops | bytes accessed | tf_op | source)
XLA Modules:
  0.0 131.9 jit_solution(11842170488230464435)
XLA Ops:
  1.3 23.1 %gather_lanes.1 = (bf16[16,64,256]{2,1,0:T(8,128)(2,1)}, bf16[16,64,256]{2,1,0:T(8,128)(2,1)}, bf16[256,2048]{1,0:T(8,128)(2,1)}, bf16[256,2048]{1,0:T(8,128)(2,1)}) custom-call(bf16[64,256]{1,0:T(8,128)(2,1)} %bitcast.24, bf16[64,256]{1,0:T(8,128)(2,1)} %bitcast.25, bf16[2048,256]{1,0:T(8,128)(2,1)} %bitcast.13, bf16[2048,256]{1,0:T(8,128)(2,1)} %bitcast.16), custom_call_target="tpu_custom_call" | custom-call | tf_op jit(solution)/shard_map/gather_lanes/pallas_call | solution.py:363
  24.4 7.5 %forward_pairs.1 = (bf16[16,128,128]{2,1,0:T(8,128)(2,1)}, f32[16,8,128]{2,1,0:T(8,128)}) custom-call(s32[1,28]{1,0:T(1,128)} %bitcast.30, s32[1,1]{1,0:T(1,128)S(6)} %copy.14.count, bf16[1024,256]{1,0:T(8,128)(2,1)} %bitcast.18, bf16[2048,256]{1,0:T(8,128)(2,1)} %bitcast.14, bf16[256,2048]{1,0:T(8,128)(2,1)} %get-tuple-element.19.vt_ref), custom_call_target="tpu_custom_call" | custom-call | tf_op jit(solution)/shard_map/forward_pairs/pallas_call | solution.py:374
  31.9 21.3 %combine_rows.1 = (bf16[64,256]{1,0:T(8,128)(2,1)}, f32[16,8,128]{2,1,0:T(8,128)}) custom-call(bf16[16,128,128]{2,1,0:T(8,128)(2,1)} %get-tuple-element.20.part, f32[16,8,128]{2,1,0:T(8,128)} %get-tuple-element.21.stat, bf16[1024,256]{1,0:T(8,128)(2,1)} %bitcast.20), custom_call_target="tpu_custom_call" | custom-call | tf_op jit(solution)/shard_map/combine_rows/pallas_call | solution.py:388
  53.2 11.8 %backward_pairs.1 = (bf16[16,128,128]{2,1,0:T(8,128)(2,1)}, bf16[2048,256]{1,0:T(8,128)(2,1)}, bf16[2048,256]{1,0:T(8,128)(2,1)}) custom-call(s32[1,28]{1,0:T(1,128)} %bitcast.31, s32[1,1]{1,0:T(1,128)S(6)} %copy.14.count, bf16[1024,256]{1,0:T(8,128)(2,1)} %bitcast.19, bf16[1024,256]{1,0:T(8,128)(2,1)} %bitcast.21, bf16[2048,256]{1,0:T(8,128)(2,1)} %bitcast.15, ...), custom_call_target="tpu_custom_call" | custom-call | tf_op jit(solution)/shard_map/backward_pairs/pallas_call | solution.py:407
  65.0 0.0 copy-start
  65.0 64.0 %reduce_gradients.1 = (bf16[64,256]{1,0:T(8,128)(2,1)}, bf16[64,256]{1,0:T(8,128)(2,1)}, bf16[64,256]{1,0:T(8,128)(2,1)}) custom-call(bf16[16,128,128]{2,1,0:T(8,128)(2,1)} %get-tuple-element.26.dq, bf16[16,2,64,256]{3,2,1,0:T(8,128)(2,1)} %bitcast.22, bf16[16,2,64,256]{3,2,1,0:T(8,128)(2,1)} %bitcast.23), custom_call_target="tpu_custom_call" | custom-call | tf_op jit(solution)/shard_map/reduce_gradients/pallas_call | solution.py:424
  128.9 0.0 copy-done
  128.9 0.0 copy-start.3
  128.9 0.6 copy.15
  129.6 0.1 copy-done.3
  129.7 0.0 copy-start.2
  129.7 0.6 copy.16
  130.3 0.2 copy-done.2
  130.5 0.0 copy-start.1
  130.5 0.6 copy.17
  131.1 0.2 copy-done.1
  131.2 0.6 copy.18
Async XLA Ops:
  65.0 64.0 %copy-start = (bf16[64,256]{1,0:T(8,128)(2,1)S(1)}, bf16[64,256]{1,0:T(8,128)(2,1)}, u32[]{:S(2)}) copy-start(bf16[64,256]{1,0:T(8,128)(2,1)} %get-tuple-element.23) | copy-start | bytes 98308
  128.9 0.8 copy-start.3
  129.7 0.8 copy-start.2
  130.5 0.8 copy-start.1

commit v2 on v1

v2 whole, which is shorter than its diff:
```python
import functools
import math

import jax
import jax.numpy as jnp
from jax import lax
from jax.experimental import pallas as pl
from jax.experimental.pallas import tpu as pltpu
from jax.sharding import PartitionSpec as P

D = 256
H = 8
HD = 32
BLK = 128
HALF = D // 2
HH = H // 2
NX = 4
TOGETHER = 4
MESH = pl.DeviceIdType.MESH
SCALE = 1.0 / math.sqrt(HD)
LOG2E = math.log2(math.e)
SCALE2 = SCALE * LOG2E
NEG = -1e30
VMEM_LIMIT = 56 * 1024 * 1024

vmem = pl.BlockSpec(memory_space=pltpu.VMEM)
smem = pl.BlockSpec(memory_space=pltpu.SMEM)


def call(kernel, name, out_shape, n_smem, n_vmem, scratch, collective_id=None):
    return pl.pallas_call(
        kernel,
        name=name,
        out_shape=out_shape,
        in_specs=[smem] * n_smem + [vmem] * n_vmem,
        out_specs=jax.tree.map(lambda _: vmem, out_shape),
        scratch_shapes=scratch,
        compiler_params=pltpu.CompilerParams(
            collective_id=collective_id,
            has_side_effects=collective_id is not None,
            vmem_limit_bytes=VMEM_LIMIT,
        ),
    )


def meet(peers):
    barrier = pltpu.get_barrier_semaphore()
    for peer in peers:
        pl.semaphore_signal(barrier, inc=1, device_id=peer, device_id_type=MESH)
    pl.semaphore_wait(barrier, len(peers))


def remote(src, dst, send_sem, recv_sem, device):
    return pltpu.make_async_remote_copy(
        src_ref=src,
        dst_ref=dst,
        send_sem=send_sem,
        recv_sem=recv_sem,
        device_id=device,
        device_id_type=MESH,
    )


def others(me, n):
    return [lax.rem(me + k, n) for k in range(1, n)]


def block_diagonal(pairs):
    blocks = pairs[0][1].shape[0] - 1
    lane = lax.broadcasted_iota(jnp.int32, (BLK, HALF), 1)
    masks = [
        jnp.where((lane >= h * HD) & (lane < (h + 1) * HD), 1.0, 0.0).astype(jnp.bfloat16)
        for h in range(HH)
    ]

    def one(b, carry):
        rows = pl.ds(pl.multiple_of(b * BLK, BLK), BLK)
        for ref, out in pairs:
            block = ref[rows, :]
            for h in range(HH):
                out[b, h * BLK : (h + 1) * BLK, :] = block * masks[h]
        return carry

    lax.fori_loop(0, blocks, one, 0)
    for _, out in pairs:
        out[blocks] = jnp.zeros(out.shape[1:], out.dtype)


def interleave(a, b):
    low = lax.broadcasted_iota(jnp.int32, a.shape, 1) < BLK // 2
    turned_a, turned_b = pltpu.roll(a, BLK // 2, 1), pltpu.roll(b, BLK // 2, 1)
    return jnp.where(low, a, turned_b), jnp.where(low, turned_a, b)


def dot_nt(a, b):
    return lax.dot_general(a, b, (((1,), (1,)), ((), ())), preferred_element_type=jnp.float32)


def dot(a, b):
    return jnp.dot(a, b, preferred_element_type=jnp.float32)


def half_at(h):
    return pl.ds(pl.multiple_of(h * HALF, HALF), HALF)


def gather_kernel(
    n_col, q_ref, g_ref, k_ref, v_ref, cells, count, qo, go, kh, vh, kt, vt, gt, info, swap_sems, sems
):
    row, me = lax.axis_index("row"), lax.axis_index("col")
    h, y, x = lax.rem(row, 2), me // NX, lax.rem(me, NX)
    ny = n_col // NX
    sibling = (row + 1 - 2 * h, me)
    along_x = [(row, y * NX + p) for p in others(x, NX)]
    along_y = [(row, p * NX + x) for p in others(y, ny)]
    meet([sibling] + along_x + along_y)
    info[h] = jnp.zeros(info.shape[1:], info.dtype)
    info[h, 0:1, 0 : cells.shape[1]] = cells[...]
    info[h, 1:2, 0:1] = count[...]
    swaps = [
        remote(src, dst, swap_sems.at[0, i], swap_sems.at[1, i], sibling)
        for i, (src, dst) in enumerate(
            (
                (q_ref.at[:, half_at(1 - h)], qo.at[h, y, x]),
                (g_ref.at[:, half_at(1 - h)], go.at[h, y, x]),
                (info.at[h], info.at[h]),
            )
        )
    ]
    for copy in swaps:
        copy.start()
    qo[h, y, x] = q_ref[:, half_at(h)]
    go[h, y, x] = g_ref[:, half_at(h)]

    def send(i, ref, peers):
        for p in peers:
            remote(ref, ref, sems.at[0, i], sems.at[1, i], p).start()

    def all_of(i, ref):
        return remote(ref, ref, sems.at[0, i], sems.at[1, i], sibling)

    def turn(src, out, turned):
        def one(b, carry):
            rows = pl.ds(pl.multiple_of(b * BLK, BLK), BLK)
            block = src[rows, half_at(h)]
            out[rows, :] = block
            turned[:, rows] = block.T
            return carry

        lax.fori_loop(0, src.shape[0] // BLK, one, 0)

    swaps[0].wait_recv()
    send(0, qo.at[:, y, x], along_x)
    swaps[1].wait_recv()
    send(1, go.at[:, y, x], along_y)
    gt[...] = go[:, y, x].reshape(BLK, HALF).T
    turn(k_ref, kh, kt)
    phases = [qo.at[:, y, 0 : NX - 1], go.at[:, 0 : ny - 1, x], qo.at[:, 0 : ny - 1], go.at[:, :, 0 : NX - 1]]
    all_of(0, phases[0]).wait_recv()
    send(2, qo.at[:, y], along_y)
    all_of(1, phases[1]).wait_recv()
    send(3, go.at[:, :, x], along_x)
    turn(v_ref, vh, vt)
    all_of(2, phases[2]).wait_recv()
    all_of(3, phases[3]).wait_recv()
    swaps[2].wait_recv()
    for i, ref in enumerate(phases):
        all_of(i, ref).wait_send()
    for copy in swaps:
        copy.wait_send()


def each_pair(info, key_blocks, q_blocks, together, visit):
    n_first = info[0, 1, 0]
    n_pairs = n_first + info[1, 1, 0]

    def group(i, carry):
        found = []
        for u in range(together):
            j = i * together + u
            second = (j >= n_first).astype(jnp.int32)
            real = j < n_pairs
            cell = info[second, 0, jnp.where(real, j - second * n_first, 0)]
            block = jnp.where(real, cell // key_blocks + second * q_blocks, 2 * q_blocks)
            q_at = pl.ds(pl.multiple_of(block * BLK, BLK), BLK)
            k_at = pl.ds(pl.multiple_of(cell % key_blocks * BLK, BLK), BLK)
            found.append((block, q_at, k_at))
        visit(found)
        return carry

    lax.fori_loop(0, (n_pairs + together - 1) // together, group, 0)


def head(h):
    return slice(h * BLK, (h + 1) * BLK), slice(h * HD, (h + 1) * HD)


def forward_kernel(key_blocks, info, q_ref, k_ref, vt_ref, part, stat, qbd, acc, top, tot):
    blocks = qbd.shape[0] - 1
    block_diagonal(((q_ref, qbd),))
    acc[...] = jnp.zeros_like(acc)
    tot[...] = jnp.zeros_like(tot)
    top[...] = jnp.full_like(top, NEG)

    def visit(pairs):
        scores = [dot_nt(k_ref[k_at, :], qbd[block]) for block, _, k_at in pairs]
        probs, fades, sums = [], [], []
        for (_, q_at, _), score in zip(pairs, scores):
            best = [jnp.max(score[:, head(h)[0]], axis=0, keepdims=True) for h in range(HH)]
            old = top[:, q_at]
            new = jnp.maximum(old, jnp.concatenate(best, axis=0) * SCALE2)
            top[:, q_at] = new
            fades.append(jnp.exp2(old - new))
            prob = [jnp.exp2(score[:, head(h)[0]] * SCALE2 - new[h : h + 1]) for h in range(HH)]
            sums.append([jnp.sum(p, axis=0, keepdims=True) for p in prob])
            probs.append([p.astype(jnp.bfloat16) for p in prob])
        mixed = [
            [dot(vt_ref[head(h)[1], k_at], prob[h]) for h in range(HH)]
            for (_, _, k_at), prob in zip(pairs, probs)
        ]
        for (_, q_at, _), fade, total, mix in zip(pairs, fades, sums, mixed):
            tot[:, q_at] = tot[:, q_at] * fade + jnp.concatenate(total, axis=0)
            for h in range(HH):
                at = head(h)[1]
                acc[at, q_at] = acc[at, q_at] * fade[h : h + 1] + mix[h]

    each_pair(info, key_blocks, blocks // 2, TOGETHER, visit)
    for b in range(blocks // 2):
        first = slice(b * BLK, (b + 1) * BLK)
        second = slice((b + blocks // 2) * BLK, (b + blocks // 2 + 1) * BLK)
        low, high = interleave(acc[:, first], acc[:, second])
        part[2 * b] = low.astype(jnp.bfloat16)
        part[2 * b + 1] = high.astype(jnp.bfloat16)
        stat[2 * b], stat[2 * b + 1] = interleave(
            jnp.concatenate([top[:, first], tot[:, first]], axis=0),
            jnp.concatenate([top[:, second], tot[:, second]], axis=0),
        )


def swap_rows(tile, out, mine, got, sems, h, sibling):
    rows = BLK // 2
    mine[...] = tile.astype(mine.dtype)
    copy = remote(
        mine.at[pl.ds(pl.multiple_of((1 - h) * rows, rows), rows)], got, sems.at[0], sems.at[1], sibling
    )
    copy.start()

    def finish():
        out[:, half_at(h)] = mine[pl.ds(pl.multiple_of(h * rows, rows), rows), :]
        copy.wait_recv()
        out[:, half_at(1 - h)] = got[...]
        copy.wait_send()

    return finish


def combine_kernel(n, part, stat, gt, att, logs, parts, stats, mine, got, sems, swap_sems):
    row, me = lax.axis_index("row"), lax.axis_index("col")
    h = lax.rem(row, 2)
    sibling = (row + 1 - 2 * h, me)
    peers = others(me, n)
    meet([sibling] + [(row, p) for p in peers])

    def send(i, src, dst, p):
        remote(src, dst, sems.at[0, i], sems.at[1, i], (row, p)).start()

    def all_of(i, ref):
        ref = ref.at[0 : n - 1]
        return remote(ref, ref, sems.at[0, i], sems.at[1, i], sibling)

    for p in peers:
        send(0, stat.at[p], stats.at[me], p)
    for p in peers:
        send(1, part.at[p], parts.at[me], p)
    grad = gt[...].astype(jnp.float32).reshape(HH, HD, BLK)
    stats[me] = stat[me]
    parts[me] = part[me]
    all_of(0, stats).wait_recv()
    every = stats[...]
    top = jnp.max(every[:, :HH], axis=0)
    fade = jnp.exp2(every[:, :HH] - top[None])
    tot = jnp.sum(every[:, HH:] * fade, axis=0)
    fade = fade / tot[None]
    all_of(1, parts).wait_recv()
    normed = jnp.zeros((HH, HD, BLK), jnp.float32)
    for p in range(n):
        normed = normed + parts[p].astype(jnp.float32).reshape(HH, HD, BLK) * fade[p][:, None, :]
    dots = jnp.sum(grad * normed, axis=1)
    logs[me] = jnp.concatenate([top + jnp.log(tot) * LOG2E, dots], axis=0)
    for p in peers:
        send(2, logs.at[me], logs.at[me], p)
    finish = swap_rows(normed.reshape(HALF, BLK).T, att, mine, got, swap_sems, h, sibling)
    all_of(0, stats).wait_send()
    all_of(1, parts).wait_send()
    finish()
    all_of(2, logs).wait_recv()
    all_of(2, logs).wait_send()


def backward_kernel(
    key_blocks, info, q_ref, g_ref, k_ref, v_ref, kt_ref, logs, att_in,
    dq, dkv, att, qbd, gbd, turned, dq_acc, dk_acc, dv_acc
):
    blocks = qbd.shape[0] - 1
    att[...] = att_in[...]
    block_diagonal(((q_ref, qbd), (g_ref, gbd)))
    dq_acc[...] = jnp.zeros_like(dq_acc)
    dk_acc[...] = jnp.zeros_like(dk_acc)
    dv_acc[...] = jnp.zeros_like(dv_acc)
    turned[blocks] = jnp.zeros(turned.shape[1:], turned.dtype)
    for b in range(blocks // 2):
        turned[b], turned[b + blocks // 2] = interleave(logs[2 * b], logs[2 * b + 1])

    def visit(pairs):
        scores = [dot_nt(k_ref[k_at, :], qbd[block]) for block, _, k_at in pairs]
        dprobs = [dot_nt(v_ref[k_at, :], gbd[block]) for block, _, k_at in pairs]
        all_weights, all_dscore = [], []
        for (block, _, _), score, dprob in zip(pairs, scores, dprobs):
            log = turned[block]
            weights, dscore = [], []
            for h in range(HH):
                lanes = head(h)[0]
                w = jnp.exp2(score[:, lanes] * SCALE2 - log[h : h + 1])
                d = w * (dprob[:, lanes] - log[HH + h : HH + h + 1])
                weights.append(w.astype(jnp.bfloat16))
                dscore.append(d.astype(jnp.bfloat16))
            all_weights.append(weights)
            all_dscore.append(dscore)
        new_v = [
            dot(jnp.concatenate(weights, axis=1), gbd[block])
            for (block, _, _), weights in zip(pairs, all_weights)
        ]
        new_k = [
            dot(jnp.concatenate(dscore, axis=1), qbd[block])
            for (block, _, _), dscore in zip(pairs, all_dscore)
        ]
        new_q = [
            [dot(kt_ref[head(h)[1], k_at], dscore[h]) for h in range(HH)]
            for (_, _, k_at), dscore in zip(pairs, all_dscore)
        ]
        for (_, q_at, k_at), vs, ks, qs in zip(pairs, new_v, new_k, new_q):
            dv_acc[k_at, :] += vs
            dk_acc[k_at, :] += ks
            for h in range(HH):
                dq_acc[head(h)[1], q_at] += qs[h]

    each_pair(info, key_blocks, blocks // 2, TOGETHER, visit)
    for b in range(blocks // 2):
        first = slice(b * BLK, (b + 1) * BLK)
        second = slice((b + blocks // 2) * BLK, (b + blocks // 2 + 1) * BLK)
        low, high = interleave(dq_acc[:, first] * SCALE, dq_acc[:, second] * SCALE)
        dq[2 * b // NX, 2 * b % NX] = low.astype(jnp.bfloat16)
        dq[(2 * b + 1) // NX, (2 * b + 1) % NX] = high.astype(jnp.bfloat16)

    def finish(b, carry):
        at = pl.ds(pl.multiple_of(b * BLK, BLK), BLK)
        dkv[b, 0] = (dk_acc[at, :] * SCALE).astype(jnp.bfloat16)
        dkv[b, 1] = dv_acc[at, :].astype(jnp.bfloat16)
        return carry

    lax.fori_loop(0, dkv.shape[0], finish, 0)


def chains(n):
    up, down = n // 2, n - 1 - n // 2
    found = []
    for sign, far in ((1, up), (-1, down)):
        for first in (far, far - 1):
            if first > 0:
                found.append((sign, list(range(first, 0, -2))))
    return found


def reduce_kernel(
    n_col, n_z, dq, dkv, out_q, out_k, out_v, first, middle, last, mine, got, sent, come,
    phase_sems, swap_sems, send_sem, come_sems
):
    row, me = lax.axis_index("row"), lax.axis_index("col")
    z, h, y, x = row // 2, lax.rem(row, 2), me // NX, lax.rem(me, NX)
    ny = n_col // NX
    sibling = (row + 1 - 2 * h, me)
    xs, ys = others(x, NX), others(y, ny)
    ring = chains(n_z)

    def at_z(delta):
        return (lax.rem(z + n_z + delta, n_z) * 2 + h, me)

    steps = sorted({sign * min(o, 2) for sign, senders in ring for o in senders})
    meet(
        [sibling]
        + [(row, y * NX + p) for p in xs]
        + [(row, p * NX + x) for p in ys]
        + [at_z(s) for s in sorted(set(steps + [-s for s in steps]))]
    )
    n_sent = sum(len(senders) for _, senders in ring)
    slots = {}

    def arrived(c, s):
        ref = come.at[slots[c, s]]
        remote(ref, ref, send_sem, come_sems.at[slots[c, s]], sibling).wait_recv()
        return come[slots[c, s]].astype(jnp.float32)

    def pass_on(s):
        for c, (sign, senders) in enumerate(ring):
            if s >= len(senders):
                continue
            slot = len(slots)
            slots[c, s] = slot
            target = lax.rem(z + n_z + sign * senders[s], n_z)
            if s == 0:
                src = dkv.at[target]
            else:
                src = sent.at[slot]
                sent[slot] = (dkv[target].astype(jnp.float32) + arrived(c, s - 1)).astype(jnp.bfloat16)
            remote(
                src, come.at[slot], send_sem, come_sems.at[slot], at_z(sign * min(senders[s], 2))
            ).start()

    def phase(i, ref):
        return remote(ref, ref, phase_sems.at[0, i], phase_sems.at[1, i], sibling)

    pass_on(0)
    for p in xs:
        remote(
            dq.at[:, p], first.at[x], phase_sems.at[0, 0], phase_sems.at[1, 0], (row, y * NX + p)
        ).start()
    most = max(len(senders) for _, senders in ring)
    finishes = []
    for s in range(1, max(most, 3)):
        if s < most:
            pass_on(s)
        if s == 1:
            first[x] = dq[:, x]
            phase(0, first.at[0 : NX - 1]).wait_recv()
            for b in range(ny):
                total = first[0, b].astype(jnp.float32)
                for k in range(1, NX):
                    total = total + first[k, b].astype(jnp.float32)
                middle[b] = total.astype(jnp.bfloat16)
            for p in ys:
                remote(
                    middle.at[p], last.at[y], phase_sems.at[0, 1], phase_sems.at[1, 1], (row, p * NX + x)
                ).start()
        if s == 2:
            last[y] = middle[y]
            phase(1, last.at[0 : ny - 1]).wait_recv()
            total = last[0].astype(jnp.float32)
            for k in range(1, ny):
                total = total + last[k].astype(jnp.float32)
            finishes.append(swap_rows(total.T, out_q, mine.at[0], got.at[0], swap_sems.at[0], h, sibling))
    total = dkv[z].astype(jnp.float32)
    for c, (_, senders) in enumerate(ring):
        total = total + arrived(c, len(senders) - 1)
    for i, out in enumerate((out_k, out_v)):
        finishes.append(
            swap_rows(total[i], out, mine.at[i + 1], got.at[i + 1], swap_sems.at[i + 1], h, sibling)
        )
    for finish in finishes:
        finish()
    ref = come.at[0:n_sent]
    remote(ref, ref, send_sem, come_sems.at[0], sibling).wait_send()
    phase(0, first.at[0 : NX - 1]).wait_send()
    phase(1, last.at[0 : ny - 1]).wait_send()


def leave_kernel(*refs):
    half = len(refs) // 2
    for src, dst in zip(refs[:half], refs[half:]):
        dst[0] = src[...]


def fwd_scratch(blocks):
    bf16, f32 = jnp.bfloat16, jnp.float32
    rows = blocks * BLK
    return [
        pltpu.VMEM((blocks + 1, HH * BLK, HALF), bf16),
        pltpu.VMEM((HALF, rows + BLK), f32),
        pltpu.VMEM((HH, rows + BLK), f32),
        pltpu.VMEM((HH, rows + BLK), f32),
    ]


def bwd_scratch(blocks, lanes):
    bf16, f32 = jnp.bfloat16, jnp.float32
    rows = blocks * BLK
    return [
        pltpu.VMEM((blocks + 1, HH * BLK, HALF), bf16),
        pltpu.VMEM((blocks + 1, HH * BLK, HALF), bf16),
        pltpu.VMEM((blocks + 1, H, BLK), f32),
        pltpu.VMEM((HALF, rows + BLK), f32),
        pltpu.VMEM((lanes, HALF), f32),
        pltpu.VMEM((lanes, HALF), f32),
    ]


def shards(n_row, n_col, queries, key_lanes, values, grad_out, pattern, counts):
    bf16, f32 = jnp.bfloat16, jnp.float32
    dma = pltpu.SemaphoreType.DMA
    shape = jax.ShapeDtypeStruct
    own_q, own_g, keys, vals = queries[0], grad_out[0], key_lanes[0], values[0]
    own_rows, lanes = own_q.shape[0], keys.shape[0]
    rows = own_rows * n_col * 2
    blocks, key_blocks, n_z, ny = rows // BLK, lanes // BLK, n_row // 2, n_col // NX

    all_q, all_g, kh, vh, kt, vt, gt, info = call(
        functools.partial(gather_kernel, n_col),
        "gather_lanes",
        (shape((2, ny, NX, own_rows, HALF), bf16),) * 2
        + (shape((lanes, HALF), bf16),) * 2
        + (shape((HALF, lanes), bf16),) * 2
        + (shape((HALF, BLK), bf16), shape((2, 8, BLK), jnp.int32)),
        0,
        6,
        [dma((2, 3)), dma((2, 4))],
        0,
    )(own_q, own_g, keys, vals, pattern[0], counts)
    all_q, all_g = all_q.reshape(rows, HALF), all_g.reshape(rows, HALF)

    part, stat = call(
        functools.partial(forward_kernel, key_blocks),
        "forward_pairs",
        (shape((n_col, HALF, BLK), bf16), shape((n_col, H, BLK), f32)),
        1,
        3,
        fwd_scratch(blocks),
    )(info, all_q, kh, vt)

    attended, logs = call(
        functools.partial(combine_kernel, n_col),
        "combine_rows",
        (shape((own_rows, D), bf16), shape((n_col, H, BLK), f32)),
        0,
        3,
        [
            pltpu.VMEM((n_col, HALF, BLK), bf16),
            pltpu.VMEM((n_col, H, BLK), f32),
            pltpu.VMEM((BLK, HALF), bf16),
            pltpu.VMEM((own_rows, HALF), bf16),
            dma((2, 3)),
            dma((2,)),
        ],
        1,
    )(part, stat, gt)

    dq, dkv, attended = call(
        functools.partial(backward_kernel, key_blocks),
        "backward_pairs",
        (
            shape((ny, NX, HALF, BLK), bf16),
            shape((key_blocks, 2, BLK, HALF), bf16),
            shape((own_rows, D), bf16),
        ),
        1,
        7,
        bwd_scratch(blocks, lanes),
    )(info, all_q, all_g, kh, vh, kt, logs, attended)

    n_sent = sum(len(senders) for _, senders in chains(n_z))
    grads = call(
        functools.partial(reduce_kernel, n_col, n_z),
        "reduce_gradients",
        (shape((own_rows, D), bf16),) * 3,
        0,
        2,
        [
            pltpu.VMEM((NX, ny, HALF, BLK), bf16),
            pltpu.VMEM((ny, HALF, BLK), bf16),
            pltpu.VMEM((ny, HALF, BLK), bf16),
            pltpu.VMEM((3, BLK, HALF), bf16),
            pltpu.VMEM((3, own_rows, HALF), bf16),
            pltpu.VMEM((n_sent, 2, BLK, HALF), bf16),
            pltpu.VMEM((n_sent, 2, BLK, HALF), bf16),
            dma((2, 2)),
            dma((3, 2)),
            dma,
            dma((n_sent,)),
        ],
        2,
    )(dq, dkv)
    grads = call(leave_kernel, "leave", (shape((1, own_rows, D), bf16),) * 3, 0, 3, [])(*grads)
    return (attended[None], *grads)


def solution(mesh):
    return jax.shard_map(
        functools.partial(shards, mesh.shape["row"], mesh.shape["col"]),
        mesh=mesh,
        in_specs=(
            P("row", "col", None),
            P("col", None, None),
            P("col", None, None),
            P("row", "col", None),
            P("row", "col", None),
            P("row", "col"),
        ),
        out_specs=(
            P("row", "col", None),
            P("row", "col", None),
            P("col", "row", None),
            P("col", "row", None),
        ),
        check_vma=False,
    )
```

time: 132 us -> 106 us (0.80)
  the two profiles are of different devices: /device:TPU:32 before, /device:TPU:1 now
where the time goes in v2:
time: 106 us
  Pallas kernels  104 us (98%)
  between operations  1.3 us (1%)
    pallas_call x1, Pallas kernels, shards(): call(functools.partial(reduce_kernel, n_col, n_z), 'reduce_gradients', (s...  47.6 us
    pallas_call x1, Pallas kernels, shards(): call(functools.partial(gather_kernel, n_col), 'gather_lanes', (shape((2,...  24.1 us
    pallas_call x1, Pallas kernels, shards(): call(functools.partial(combine_kernel, n_col), 'combine_rows', (shape((ow...  18.7 us
    pallas_call x1, Pallas kernels, shards(): call(functools.partial(backward_kernel, key_blocks), 'backward_pairs', (s...  7.5 us
    pallas_call x1, Pallas kernels, shards(): call(functools.partial(forward_kernel, key_blocks), 'forward_pairs', (sha...  5.04 us

profile of v2, /device:TPU:1, one launch (start us, length us, event | category | flops | bytes accessed | tf_op | source)
XLA Modules:
  0.0 105.7 jit_solution(2566941447656618753)
XLA Ops:
  1.3 24.1 %gather_lanes.1 = (bf16[2,4,4,64,128]{4,3,2,1,0:T(8,128)(2,1)}, bf16[2,4,4,64,128]{4,3,2,1,0:T(8,128)(2,1)}, bf16[2048,128]{1,0:T(8,128)(2,1)}, bf16[2048,128]{1...) custom-call(bf16[64,256]{1,0:T(8,128)(2,1)} %bitcast.13, ...), custom_call_target="tpu_custom_call" | custom-call | tf_op jit(solution)/shard_map/gather_lanes/pallas_call | solution.py:505
  25.4 5.0 %forward_pairs.1 = (bf16[16,128,128]{2,1,0:T(8,128)(2,1)}, f32[16,8,128]{2,1,0:T(8,128)}) custom-call(s32[2,8,128]{2,1,0:T(8,128)} %get-tuple-element.25.info, bf16[2048,128]{1,0:T(8,128)(2,1)} %bitcast.8, bf16[2048,128]{1,0:T(8,128)(2,1)} %get-tuple-element.28.k_ref, bf16[128,2048]{1,0:T(8,128)(2,1)} %get-tuple-element.31.vt_ref), custom_call_target="tpu_custom_call" | custom-call | tf_op jit(solution)/shard_map/forward_pairs/pallas_call | solution.py:519
  30.5 18.7 %combine_rows.1 = (bf16[64,256]{1,0:T(8,128)(2,1)}, f32[16,8,128]{2,1,0:T(8,128)}) custom-call(bf16[16,128,128]{2,1,0:T(8,128)(2,1)} %get-tuple-element.32.part, f32[16,8,128]{2,1,0:T(8,128)} %get-tuple-element.33.stat, bf16[128,128]{1,0:T(8,128)(2,1)} %get-tuple-element.34.gt), custom_call_target="tpu_custom_call" | custom-call | tf_op jit(solution)/shard_map/combine_rows/pallas_call | solution.py:528
  49.1 7.5 %backward_pairs.1 = (bf16[4,4,128,128]{3,2,1,0:T(8,128)(2,1)}, bf16[16,2,128,128]{3,2,1,0:T(8,128)(2,1)}, bf16[64,256]{1,0:T(8,128)(2,1)}) custom-call(s32[2,8,128]{2,1,0:T(8,128)} %get-tuple-element.25.info, bf16[2048,128]{1,0:T(8,128)(2,1)} %bitcast.9, bf16[2048,128]{1,0:T(8,128)(2,1)} %bitcast.12, bf16[2048,128]{1,0:T(8,128)(2,1)} %get-tuple-element.28.k_ref, ...), custom_call_target="tpu_custom_call" | custom-call | tf_op jit(solution)/shard_map/backward_pairs/pallas_call | solution.py:545
  56.6 47.6 %reduce_gradients.1 = (bf16[64,256]{1,0:T(8,128)(2,1)}, bf16[64,256]{1,0:T(8,128)(2,1)}, bf16[64,256]{1,0:T(8,128)(2,1)}) custom-call(bf16[4,4,128,128]{3,2,1,0:T(8,128)(2,1)} %get-tuple-element.38.dq, bf16[16,2,128,128]{3,2,1,0:T(8,128)(2,1)} %get-tuple-element.39.dkv), custom_call_target="tpu_custom_call" | custom-call | tf_op jit(solution)/shard_map/reduce_gradients/pallas_call | solution.py:559
  104.3 1.4 %leave.1 = (bf16[1,64,256]{2,1,0:T(8,128)(2,1)}, bf16[1,64,256]{2,1,0:T(8,128)(2,1)}, bf16[1,64,256]{2,1,0:T(8,128)(2,1)}) custom-call(bf16[64,256]{1,0:T(8,128)(2,1)} %get-tuple-element.40.refs_0_, bf16[64,256]{1,0:T(8,128)(2,1)} %get-tuple-element.41.refs_1_, bf16[64,256]{1,0:T(8,128)(2,1)} %get-tuple-element.42.refs_2_), custom_call_target="tpu_custom_call" | custom-call | tf_op jit(solution)/shard_map/leave/pallas_call | solution.py:580

commit v3 on v2

v3 whole, which is shorter than its diff:
```python
import functools
import math

import jax
import jax.numpy as jnp
from jax import lax
from jax.experimental import pallas as pl
from jax.experimental.pallas import tpu as pltpu
from jax.sharding import PartitionSpec as P

D = 256
H = 8
HD = 32
BLK = 128
HALF = D // 2
HH = H // 2
NX = 4
TOGETHER = 4
MESH = pl.DeviceIdType.MESH
SCALE = 1.0 / math.sqrt(HD)
LOG2E = math.log2(math.e)
SCALE2 = SCALE * LOG2E
NEG = -1e30
VMEM_LIMIT = 32 * 1024 * 1024

vmem = pl.BlockSpec(memory_space=pltpu.VMEM)
smem = pl.BlockSpec(memory_space=pltpu.SMEM)


def call(kernel, name, out_shape, in_specs, scratch, collective_id=None, micros=10):
    return pl.pallas_call(
        kernel,
        name=name,
        out_shape=out_shape,
        in_specs=in_specs,
        out_specs=jax.tree.map(lambda _: vmem, out_shape),
        scratch_shapes=scratch,
        cost_estimate=pl.CostEstimate(
            flops=micros * 10**9, bytes_accessed=micros * 10**6, transcendentals=0
        ),
        compiler_params=pltpu.CompilerParams(
            collective_id=collective_id,
            has_side_effects=collective_id is not None,
            vmem_limit_bytes=VMEM_LIMIT,
        ),
    )


def meet(peers):
    barrier = pltpu.get_barrier_semaphore()
    for peer in peers:
        pl.semaphore_signal(barrier, inc=1, device_id=peer, device_id_type=MESH)
    pl.semaphore_wait(barrier, len(peers))


def remote(src, dst, send_sem, recv_sem, device):
    return pltpu.make_async_remote_copy(
        src_ref=src,
        dst_ref=dst,
        send_sem=send_sem,
        recv_sem=recv_sem,
        device_id=device,
        device_id_type=MESH,
    )


def others(me, n):
    return [lax.rem(me + k, n) for k in range(1, n)]


def block_diagonal(pairs):
    blocks = pairs[0][1].shape[0] - 1
    lane = lax.broadcasted_iota(jnp.int32, (BLK, HALF), 1)
    masks = [
        jnp.where((lane >= h * HD) & (lane < (h + 1) * HD), 1.0, 0.0).astype(jnp.bfloat16)
        for h in range(HH)
    ]

    def one(b, carry):
        rows = pl.ds(pl.multiple_of(b * BLK, BLK), BLK)
        for ref, out in pairs:
            block = ref[rows, :]
            for h in range(HH):
                out[b, h * BLK : (h + 1) * BLK, :] = block * masks[h]
        return carry

    lax.fori_loop(0, blocks, one, 0, unroll=4)
    for _, out in pairs:
        out[blocks] = jnp.zeros(out.shape[1:], out.dtype)


def interleave(a, b):
    low = lax.broadcasted_iota(jnp.int32, a.shape, 1) < BLK // 2
    turned_a, turned_b = pltpu.roll(a, BLK // 2, 1), pltpu.roll(b, BLK // 2, 1)
    return jnp.where(low, a, turned_b), jnp.where(low, turned_a, b)


def dot_nt(a, b):
    return lax.dot_general(a, b, (((1,), (1,)), ((), ())), preferred_element_type=jnp.float32)


def dot(a, b):
    return jnp.dot(a, b, preferred_element_type=jnp.float32)


def half_at(h):
    return pl.ds(pl.multiple_of(h * HALF, HALF), HALF)


def turn_blocks(src, half, out):
    def one(b, carry):
        rows = pl.ds(pl.multiple_of(b * BLK, BLK), BLK)
        out[:, rows] = src[rows, half].T
        return carry

    lax.fori_loop(0, src.shape[0] // BLK, one, 0, unroll=4)


def gather_kernel(n_col, own_ref, qo, go, info, tables, swap_sems, sems):
    row, me = lax.axis_index("row"), lax.axis_index("col")
    h, y, x = lax.rem(row, 2), me // NX, lax.rem(me, NX)
    ny = n_col // NX
    rows = qo.shape[3]
    sibling = (row + 1 - 2 * h, me)
    along_x = [(row, y * NX + p) for p in others(x, NX)]
    along_y = [(row, p * NX + x) for p in others(y, ny)]
    meet([sibling] + along_x + along_y)
    swaps = [
        remote(src, dst, swap_sems.at[0, i], swap_sems.at[1, i], sibling)
        for i, (src, dst) in enumerate(
            (
                (own_ref.at[0:rows, half_at(1 - h)], qo.at[h, y, x]),
                (own_ref.at[rows : 2 * rows, half_at(1 - h)], go.at[h, y, x]),
                (own_ref.at[2 * rows :, 0:HALF], tables.at[h]),
            )
        )
    ]
    for copy in swaps:
        copy.start()
    qo[h, y, x] = own_ref[0:rows, half_at(h)]
    go[h, y, x] = own_ref[rows : 2 * rows, half_at(h)]
    tables[h] = own_ref[2 * rows :, 0:HALF]

    def send(i, ref, peers):
        for p in peers:
            remote(ref, ref, sems.at[0, i], sems.at[1, i], p).start()

    def all_of(i, ref):
        return remote(ref, ref, sems.at[0, i], sems.at[1, i], sibling)

    phases = [qo.at[:, y, 0 : NX - 1], go.at[:, 0 : ny - 1, x], qo.at[:, 0 : ny - 1], go.at[:, :, 0 : NX - 1]]
    swaps[0].wait_recv()
    send(0, qo.at[:, y, x], along_x)
    swaps[1].wait_recv()
    send(1, go.at[:, y, x], along_y)
    swaps[2].wait_recv()
    table = tables[...].astype(jnp.float32).astype(jnp.int32)
    mark = lax.broadcasted_iota(jnp.int32, table.shape, 1) == 2
    info[...] = jnp.where(mark, h, table)
    all_of(0, phases[0]).wait_recv()
    send(2, qo.at[:, y], along_y)
    all_of(1, phases[1]).wait_recv()
    send(3, go.at[:, :, x], along_x)
    all_of(2, phases[2]).wait_recv()
    all_of(3, phases[3]).wait_recv()
    for i, ref in enumerate(phases):
        all_of(i, ref).wait_send()
    for copy in swaps:
        copy.wait_send()


def each_pair(info, key_blocks, q_blocks, together, visit):
    n_first = info[0, 1, 0]
    n_pairs = n_first + info[1, 1, 0]

    def group(i, carry):
        found = []
        for u in range(together):
            j = i * together + u
            second = (j >= n_first).astype(jnp.int32)
            real = j < n_pairs
            cell = info[second, 0, jnp.where(real, j - second * n_first, 0)]
            block = jnp.where(real, cell // key_blocks + second * q_blocks, 2 * q_blocks)
            q_at = pl.ds(pl.multiple_of(block * BLK, BLK), BLK)
            k_at = pl.ds(pl.multiple_of(cell % key_blocks * BLK, BLK), BLK)
            found.append((block, q_at, k_at))
        visit(found)
        return carry

    lax.fori_loop(0, (n_pairs + together - 1) // together, group, 0)


def head(h):
    return slice(h * BLK, (h + 1) * BLK), slice(h * HD, (h + 1) * HD)


def forward_kernel(key_blocks, info, q_ref, g_ref, k_ref, v_ref, acc, stat, vt_ref, qbd, top, tot):
    own = half_at(info[0, 2, 0])
    turn_blocks(v_ref, own, vt_ref)
    blocks = qbd.shape[0] - 1
    block_diagonal(((q_ref, qbd),))
    acc[...] = jnp.zeros_like(acc)
    tot[...] = jnp.zeros_like(tot)
    top[...] = jnp.full_like(top, NEG)

    def visit(pairs):
        scores = [dot_nt(k_ref[k_at, own], qbd[block]) for block, _, k_at in pairs]
        probs, fades, sums = [], [], []
        for (_, q_at, _), score in zip(pairs, scores):
            best = [jnp.max(score[:, head(h)[0]], axis=0, keepdims=True) for h in range(HH)]
            old = top[:, q_at]
            new = jnp.maximum(old, jnp.concatenate(best, axis=0) * SCALE2)
            top[:, q_at] = new
            fades.append(jnp.exp2(old - new))
            prob = [jnp.exp2(score[:, head(h)[0]] * SCALE2 - new[h : h + 1]) for h in range(HH)]
            sums.append([jnp.sum(p, axis=0, keepdims=True) for p in prob])
            probs.append([p.astype(jnp.bfloat16) for p in prob])
        mixed = [
            [dot(vt_ref[head(h)[1], k_at], prob[h]) for h in range(HH)]
            for (_, _, k_at), prob in zip(pairs, probs)
        ]
        for (_, q_at, _), fade, total, mix in zip(pairs, fades, sums, mixed):
            tot[:, q_at] = tot[:, q_at] * fade + jnp.concatenate(total, axis=0)
            for h in range(HH):
                at = head(h)[1]
                acc[at, q_at] = acc[at, q_at] * fade[h : h + 1] + mix[h]

    each_pair(info, key_blocks, blocks // 2, TOGETHER, visit)
    lanes = blocks // 2 * BLK
    for b in range(blocks):
        r, at = divmod(b, blocks // 2)
        from_lane, to_lane = b * BLK, at * BLK
        grad = g_ref[from_lane : from_lane + BLK, :].astype(jnp.float32).T
        dots = jnp.sum((grad * acc[:, from_lane : from_lane + BLK]).reshape(HH, HD, BLK), axis=1)
        stat[r, 0:HH, to_lane : to_lane + BLK] = top[:, from_lane : from_lane + BLK]
        stat[r, HH:H, to_lane : to_lane + BLK] = tot[:, from_lane : from_lane + BLK]
        fold, to_lane = divmod(to_lane, lanes // 2)
        stat[r, fold * HH : (fold + 1) * HH, lanes + to_lane : lanes + to_lane + BLK] = dots


def swap_rows(tile, out, mine, got, sems, h, sibling):
    rows = BLK // 2
    mine[...] = tile.astype(mine.dtype)
    copy = remote(
        mine.at[pl.ds(pl.multiple_of((1 - h) * rows, rows), rows)], got, sems.at[0], sems.at[1], sibling
    )
    copy.start()

    def finish():
        out[:, half_at(h)] = mine[pl.ds(pl.multiple_of(h * rows, rows), rows), :]
        copy.wait_recv()
        out[:, half_at(1 - h)] = got[...]
        copy.wait_send()

    return finish


def combine_kernel(n, stat, logs, got, middle, sems):
    row, me = lax.axis_index("row"), lax.axis_index("col")
    y, x = me // NX, lax.rem(me, NX)
    ny = n // NX
    lanes = stat.shape[2] * 2 // 3
    along_x = (x, NX, [(row, y * NX + p) for p in others(x, NX)])
    along_y = (y, ny, [(row, p * NX + x) for p in others(y, ny)])
    meet(along_x[2] + along_y[2])

    def start(phase, r, src):
        here, _, peers = (along_x, along_y)[phase ^ r]
        for p in peers:
            dst = got.at[phase, r, here]
            remote(src, dst, sems.at[0, phase, r], sems.at[1, phase, r], p).start()
        got[phase, r, here] = src[...]

    def all_of(phase, r):
        _, size, peers = (along_x, along_y)[phase ^ r]
        ref = got.at[phase, r, 0 : size - 1]
        return remote(ref, ref, sems.at[0, phase, r], sems.at[1, phase, r], peers[0])

    def merged(phase, r):
        size = (along_x, along_y)[phase ^ r][1]
        parts = [got[phase, r, i] for i in range(size)]
        top = functools.reduce(jnp.maximum, [part[0:HH, :lanes] for part in parts])
        tot, dots = 0.0, 0.0
        for part in parts:
            fade = jnp.exp2(part[0:HH, :lanes] - top)
            tot = tot + part[HH:H, :lanes] * fade
            fold = jnp.concatenate([fade[:, : lanes // 2], fade[:, lanes // 2 :]], axis=0)
            dots = dots + part[:, lanes:] * fold
        return top, tot, dots

    for r in range(2):
        start(0, r, stat.at[r])
    for r in range(2):
        all_of(0, r).wait_recv()
        top, tot, dots = merged(0, r)
        middle[r, 0:HH, :lanes] = top
        middle[r, HH:H, :lanes] = tot
        middle[r, :, lanes:] = dots
        start(1, r, middle.at[r])
    for r in range(2):
        all_of(1, r).wait_recv()
        top, tot, dots = merged(1, r)
        total = top + jnp.log(tot) * LOG2E
        dots = jnp.concatenate([dots[0:HH], dots[HH:H]], axis=1) / tot
        for b in range(lanes // BLK):
            at = slice(b * BLK, (b + 1) * BLK)
            logs[r * (lanes // BLK) + b, 0:HH] = total[:, at]
            logs[r * (lanes // BLK) + b, HH:H] = dots[:, at]
    for phase in range(2):
        for r in range(2):
            all_of(phase, r).wait_send()


def backward_kernel(
    key_blocks, info, q_ref, g_ref, k_ref, v_ref, logs_ref, weighted, stat,
    tiles, dkv, kt_ref, qbd, gbd, logs, dq_acc, dk_acc, dv_acc
):
    blocks = qbd.shape[0] - 1
    own = half_at(info[0, 2, 0])
    turn_blocks(k_ref, own, kt_ref)
    block_diagonal(((q_ref, qbd), (g_ref, gbd)))
    dq_acc[...] = jnp.zeros_like(dq_acc)
    dk_acc[...] = jnp.zeros_like(dk_acc)
    dv_acc[...] = jnp.zeros_like(dv_acc)
    logs[0:blocks] = logs_ref[...]
    logs[blocks] = jnp.zeros(logs.shape[1:], logs.dtype)

    def visit(pairs):
        scores = [dot_nt(k_ref[k_at, own], qbd[block]) for block, _, k_at in pairs]
        dprobs = [dot_nt(v_ref[k_at, own], gbd[block]) for block, _, k_at in pairs]
        all_weights, all_dscore = [], []
        for (block, _, _), score, dprob in zip(pairs, scores, dprobs):
            log = logs[block]
            weights, dscore = [], []
            for h in range(HH):
                lanes = head(h)[0]
                w = jnp.exp2(score[:, lanes] * SCALE2 - log[h : h + 1])
                d = w * (dprob[:, lanes] - log[HH + h : HH + h + 1])
                weights.append(w.astype(jnp.bfloat16))
                dscore.append(d.astype(jnp.bfloat16))
            all_weights.append(weights)
            all_dscore.append(dscore)
        new_v = [
            dot(jnp.concatenate(weights, axis=1), gbd[block])
            for (block, _, _), weights in zip(pairs, all_weights)
        ]
        new_k = [
            dot(jnp.concatenate(dscore, axis=1), qbd[block])
            for (block, _, _), dscore in zip(pairs, all_dscore)
        ]
        new_q = [
            [dot(kt_ref[head(h)[1], k_at], dscore[h]) for h in range(HH)]
            for (_, _, k_at), dscore in zip(pairs, all_dscore)
        ]
        for (_, q_at, k_at), vs, ks, qs in zip(pairs, new_v, new_k, new_q):
            dv_acc[k_at, :] += vs
            dk_acc[k_at, :] += ks
            for h in range(HH):
                dq_acc[head(h)[1], q_at] += qs[h]

    each_pair(info, key_blocks, blocks // 2, TOGETHER, visit)
    for b in range(blocks // 2):
        at = slice(b * BLK, (b + 1) * BLK)
        grads, normed = [], []
        for r in range(2):
            block = r * (blocks // 2) + b
            lanes = slice(block * BLK, (block + 1) * BLK)
            grads.append(dq_acc[:, lanes] * SCALE)
            fade = jnp.exp2(stat[r, 0:HH, at] - logs[block, 0:HH])
            part = weighted[:, lanes].reshape(HH, HD, BLK) * fade[:, None, :]
            normed.append(part.reshape(HALF, BLK))
        for i, both in enumerate((grads, normed)):
            for k, tile in enumerate(interleave(*both)):
                tiles[i, (2 * b + k) // NX, (2 * b + k) % NX] = tile.astype(jnp.bfloat16)

    def finish(b, carry):
        at = pl.ds(pl.multiple_of(b * BLK, BLK), BLK)
        dkv[b, 0] = (dk_acc[at, :] * SCALE).astype(jnp.bfloat16)
        dkv[b, 1] = dv_acc[at, :].astype(jnp.bfloat16)
        return carry

    lax.fori_loop(0, dkv.shape[0], finish, 0, unroll=4)


def chains(n):
    up, down = n // 2, n - 1 - n // 2
    near = (up + 1) // 2
    found = []
    for first, last in ((near, 1), (up, near + 1)):
        for sign, far in ((1, up), (-1, down)):
            senders = list(range(min(first, far), last - 1, -1))
            if senders:
                found.append((sign, senders))
    return found


def reduce_kernel(
    n_col, n_z, tiles, dkv, out_q, out_k, out_v, out_a, first, middle, last, mine, got, sent, come, ended, beside,
    phase_sems, swap_sems, send_sem, come_sems, end_send, end_sems, beside_sems
):
    row, me = lax.axis_index("row"), lax.axis_index("col")
    z, h, y, x = row // 2, lax.rem(row, 2), me // NX, lax.rem(me, NX)
    ny = n_col // NX
    sibling = (row + 1 - 2 * h, me)
    xs, ys = others(x, NX), others(y, ny)
    ring = chains(n_z)
    hops = [
        [sign * (o - after) for o, after in zip(senders, senders[1:] + [0])] for sign, senders in ring
    ]

    def at_z(delta, core):
        return (lax.rem(z + n_z + delta, n_z) * 2 + core, me)

    def both_ways(deltas):
        return sorted({d % n_z for d in deltas} | {-d % n_z for d in deltas})

    def lanes_of(core):
        return pl.ds(pl.multiple_of(core * (BLK // 2), BLK // 2), BLK // 2)

    meet(
        [sibling]
        + [at_z(d, h) for d in both_ways([d for c in hops for d in c])]
        + [at_z(d, 1 - h) for d in both_ways([c[-1] for c in hops])]
        + [(row, y * NX + p) for p in xs]
        + [(row, p * NX + x) for p in ys]
    )
    slots = {}

    def arrived(i, c, s):
        slot = slots[c, s]
        ref = come.at[i, slot]
        remote(ref, ref, send_sem, come_sems.at[i, slot], sibling).wait_recv()
        return come[i, slot]

    def pass_on(s):
        for i in range(2):
            for c, (sign, senders) in enumerate(ring):
                if s >= len(senders):
                    continue
                target = lax.rem(z + n_z + sign * senders[s], n_z)
                if s == len(senders) - 1:
                    sent[i, c] = dkv[target, i] + arrived(i, c, s - 1) if s else dkv[target, i]
                    if i == 1:
                        for core in range(2):
                            remote(
                                sent.at[:, c, core * (BLK // 2) : (core + 1) * (BLK // 2)],
                                ended.at[c, h],
                                end_send,
                                end_sems.at[c, h],
                                at_z(hops[c][s], core),
                            ).start()
                    continue
                slot = slots.setdefault((c, s), len(slots))
                if s == 0:
                    src = dkv.at[target, i]
                else:
                    src = sent.at[i, len(ring) + slot]
                    sent[i, len(ring) + slot] = dkv[target, i] + arrived(i, c, s - 1)
                remote(
                    src, come.at[i, slot], send_sem, come_sems.at[i, slot], at_z(hops[c][s], h)
                ).start()

    along_x = (x, NX, [(p, (row, y * NX + p)) for p in xs])
    along_y = (y, ny, [(p, (row, p * NX + x)) for p in ys])

    def phase(i, step):
        size = (along_x, along_y)[i ^ step][1]
        ref = (first, last)[step].at[i, 0 : size - 1]
        return remote(ref, ref, phase_sems.at[0, i, step], phase_sems.at[1, i, step], sibling)

    def spread(i, step):
        here, size, peers = (along_x, along_y)[i ^ step]
        for p, device in peers:
            src = middle.at[i, p] if step else (tiles.at[0, :, p] if i == 0 else tiles.at[1, p])
            dst = (first, last)[step].at[i, here]
            remote(src, dst, phase_sems.at[0, i, step], phase_sems.at[1, i, step], device).start()
        if step:
            last[i, here] = middle[i, here]
        else:
            first[i, here] = tiles[0, :, x] if i == 0 else tiles[1, y]

    def summed(i, step, at):
        size = (along_x, along_y)[i ^ step][1]
        refs = [first[i, k, at] if step == 0 else last[i, k] for k in range(size)]
        return functools.reduce(jnp.add, [ref.astype(jnp.float32) for ref in refs])

    pass_on(0)
    aside = remote(dkv.at[z, :, lanes_of(1 - h)], beside, beside_sems.at[0], beside_sems.at[1], sibling)
    aside.start()
    for i in range(2):
        spread(i, 0)
    most = max(len(senders) for _, senders in ring)
    finishes = []
    for s in range(1, max(most, 4)):
        if s < most:
            pass_on(s)
        for i in range(2):
            if s == 2:
                phase(i, 0).wait_recv()
                for b in range((along_y, along_x)[i][1]):
                    middle[i, b] = summed(i, 0, b).astype(jnp.bfloat16)
                spread(i, 1)
            if s == 3:
                phase(i, 1).wait_recv()
                out = (out_q, out_a)[i]
                finishes.append(
                    swap_rows(summed(i, 1, 0).T, out, mine.at[i], got.at[i], swap_sems.at[i], h, sibling)
                )
    aside.wait_recv()
    for finish in finishes:
        finish()
    totals = [dkv[z, :, lanes_of(h)].astype(jnp.float32), beside[...].astype(jnp.float32)]
    for c in range(len(ring)):
        for k, core in enumerate((h, 1 - h)):
            ref = ended.at[c, core]
            remote(ref, ref, end_send, end_sems.at[c, core], sibling).wait_recv()
            totals[k] = totals[k] + ended[c, core].astype(jnp.float32)
    for total, core in zip(totals, (h, 1 - h)):
        out_k[:, half_at(core)] = total[0].astype(jnp.bfloat16)
        out_v[:, half_at(core)] = total[1].astype(jnp.bfloat16)
    aside.wait_send()
    remote(come, come, send_sem, come_sems.at[0, 0], sibling).wait_send()
    remote(ended, ended, end_send, end_sems.at[0, 0], sibling).wait_send()
    for i in range(2):
        for step in range(2):
            phase(i, step).wait_send()


def leave_kernel(*refs):
    half = len(refs) // 2
    for src, dst in zip(refs[:half], refs[half:]):
        dst[0] = src[...]


def fwd_scratch(blocks, lanes):
    bf16, f32 = jnp.bfloat16, jnp.float32
    rows = blocks * BLK
    return [
        pltpu.VMEM((HALF, lanes), bf16),
        pltpu.VMEM((blocks + 1, HH * BLK, HALF), bf16),
        pltpu.VMEM((HH, rows + BLK), f32),
        pltpu.VMEM((HH, rows + BLK), f32),
    ]


def bwd_scratch(blocks, lanes):
    bf16, f32 = jnp.bfloat16, jnp.float32
    rows = blocks * BLK
    return [
        pltpu.VMEM((HALF, lanes), bf16),
        pltpu.VMEM((blocks + 1, HH * BLK, HALF), bf16),
        pltpu.VMEM((blocks + 1, HH * BLK, HALF), bf16),
        pltpu.VMEM((blocks + 1, H, BLK), f32),
        pltpu.VMEM((HALF, rows + BLK), f32),
        pltpu.VMEM((lanes, HALF), f32),
        pltpu.VMEM((lanes, HALF), f32),
    ]


def shards(n_row, n_col, queries, key_lanes, values, grad_out, pattern, counts):
    bf16, f32 = jnp.bfloat16, jnp.float32
    dma = pltpu.SemaphoreType.DMA
    shape = jax.ShapeDtypeStruct
    own_q, own_g, keys, vals = queries[0], grad_out[0], key_lanes[0], values[0]
    own_rows, lanes = own_q.shape[0], keys.shape[0]
    rows = own_rows * n_col * 2
    blocks, key_blocks, n_z, ny = rows // BLK, lanes // BLK, n_row // 2, n_col // NX

    own_cells = jnp.pad(pattern[0].astype(bf16), ((0, 0), (0, D - pattern.shape[2])))
    own_count = jnp.pad(counts.astype(bf16), ((0, 14), (0, D - 1)))
    own = jnp.concatenate([own_q, own_g, own_cells, own_count], axis=0)
    all_q, all_g, info = call(
        functools.partial(gather_kernel, n_col),
        "gather_lanes",
        (shape((2, ny, NX, own_rows, HALF), bf16),) * 2 + (shape((2, 16, BLK), jnp.int32),),
        [vmem],
        [pltpu.VMEM((2, 16, HALF), bf16), dma((2, 3)), dma((2, 4))],
        0,
    )(own)
    all_q, all_g = all_q.reshape(rows, HALF), all_g.reshape(rows, HALF)

    folded = (H, rows // 2 * 3 // 2)
    weighted, stat = call(
        functools.partial(forward_kernel, key_blocks),
        "forward_pairs",
        (shape((HALF, rows + BLK), f32), shape((2, *folded), f32)),
        [smem] + [vmem] * 4,
        fwd_scratch(blocks, lanes),
    )(info, all_q, all_g, keys, vals)

    logs = call(
        functools.partial(combine_kernel, n_col),
        "combine_rows",
        shape((blocks, H, BLK), f32),
        [vmem],
        [
            pltpu.VMEM((2, 2, max(NX, ny), *folded), f32),
            pltpu.VMEM((2, *folded), f32),
            dma((2, 2, 2)),
        ],
        1,
    )(stat)

    tiles, dkv = call(
        functools.partial(backward_kernel, key_blocks),
        "backward_pairs",
        (shape((2, ny, NX, HALF, BLK), bf16), shape((key_blocks, 2, BLK, HALF), bf16)),
        [smem] + [vmem] * 7,
        bwd_scratch(blocks, lanes),
    )(info, all_q, all_g, keys, vals, logs, weighted, stat)

    side = max(NX, ny)
    n_chains, n_sent = len(chains(n_z)), sum(len(senders) for _, senders in chains(n_z))
    grads = call(
        functools.partial(reduce_kernel, n_col, n_z),
        "reduce_gradients",
        (shape((own_rows, D), bf16),) * 4,
        [vmem] * 2,
        [
            pltpu.VMEM((2, side, side, HALF, BLK), bf16),
            pltpu.VMEM((2, side, HALF, BLK), bf16),
            pltpu.VMEM((2, side, HALF, BLK), bf16),
            pltpu.VMEM((2, BLK, HALF), bf16),
            pltpu.VMEM((2, own_rows, HALF), bf16),
            pltpu.VMEM((2, n_sent, BLK, HALF), bf16),
            pltpu.VMEM((2, n_sent - n_chains, BLK, HALF), bf16),
            pltpu.VMEM((n_chains, 2, 2, own_rows, HALF), bf16),
            pltpu.VMEM((2, own_rows, HALF), bf16),
            dma((2, 2, 2)),
            dma((2, 2)),
            dma,
            dma((2, n_sent - n_chains)),
            dma,
            dma((n_chains, 2)),
            dma((2,)),
        ],
        2,
    )(tiles, dkv)
    grad_q, grad_k, grad_v, attended = call(
        leave_kernel, "leave", (shape((1, own_rows, D), bf16),) * 4, [vmem] * 4, []
    )(*grads)
    return attended, grad_q, grad_k, grad_v


def solution(mesh):
    return jax.shard_map(
        functools.partial(shards, mesh.shape["row"], mesh.shape["col"]),
        mesh=mesh,
        in_specs=(
            P("row", "col", None),
            P("col", None, None),
            P("col", None, None),
            P("row", "col", None),
            P("row", "col", None),
            P("row", "col"),
        ),
        out_specs=(
            P("row", "col", None),
            P("row", "col", None),
            P("col", "row", None),
            P("col", "row", None),
        ),
        check_vma=False,
    )
```

time: 106 us -> 88.3 us (0.83)
  Pallas kernels: 104 us -> 85.2 us
  other arithmetic: 0 us -> 1.44 us
    pallas_call x2, Pallas kernels: 20.1 us -> 11.1 us  [the longest x1 10.4 us: shards(): call(functools.partial(combine_kernel, n_col), 'combine_rows', shape((blo...]
    pallas_call x1, Pallas kernels: 47.6 us -> 41.7 us  [shards(): call(functools.partial(reduce_kernel, n_col, n_z), 'reduce_gradients', (s...]
    pallas_call x1, Pallas kernels: 24.1 us -> 21 us  [shards(): call(functools.partial(gather_kernel, n_col), 'gather_lanes', (shape((2,...]
where the time goes in v3:
time: 88.3 us; the launch traced here: 88 us
  Pallas kernels  85.2 us (96%)
  other arithmetic  1.44 us (2%)
  between operations  1.36 us (2%)
    pallas_call x1, Pallas kernels, shards(): call(functools.partial(reduce_kernel, n_col, n_z), 'reduce_gradients', (s...  41.7 us
    pallas_call x1, Pallas kernels, shards(): call(functools.partial(gather_kernel, n_col), 'gather_lanes', (shape((2,...  21 us
    pallas_call x1, Pallas kernels, shards(): call(functools.partial(combine_kernel, n_col), 'combine_rows', shape((blo...  10.4 us
    pallas_call x1, Pallas kernels, shards(): call(functools.partial(backward_kernel, key_blocks), 'backward_pairs', (s...  6.83 us
    pallas_call x1, Pallas kernels, shards(): call(functools.partial(forward_kernel, key_blocks), 'forward_pairs', (sha...  4.56 us

profile of v3, /device:TPU:1, one launch (start us, length us, event | category | flops | bytes accessed | tf_op | source)
XLA Modules:
  0.0 88.0 jit_solution(10639784703582691721)
XLA Ops:
  1.3 0.7 convert_bitcast_fusion
  1.9 0.8 fusion.4.own_ref
  2.7 0.0 copy-start
  2.7 0.0 copy-start.1
  2.8 21.0 %gather_lanes.1 = (bf16[2,4,4,64,128]{4,3,2,1,0:T(8,128)(2,1)S(1)}, bf16[2,4,4,64,128]{4,3,2,1,0:T(8,128)(2,1)S(1)}, s32[2,16,128]{2,1,0:T(8,128)S(1)}) custom-call(bf16[144,256]{1,0:T(8,128)(2,1)S(1)} %fusion.4.own_ref), custom_call_target="tpu_custom_call" | custom-call | flops 10000000000 | bytes 10000000 | tf_op jit(solution)/shard_map/gather_lanes/pallas_call | solution.py:572
  23.8 0.0 copy-done
  23.8 0.0 copy-done.1
  23.8 4.6 %forward_pairs.1 = (f32[128,2176]{1,0:T(8,128)S(1)}, f32[2,8,1536]{2,1,0:T(8,128)S(1)}) custom-call(s32[2,16,128]{2,1,0:T(8,128)S(1)} %get-tuple-element.19.info, bf16[2048,128]{1,0:T(8,128)(2,1)S(1)} %bitcast.12, bf16[2048,128]{1,0:T(8,128)(2,1)S(1)} %bitcast.14, bf16[2048,256]{1,0:T(8,128)(2,1)S(1)} %bitcast.8, bf16[2048,256]{1,0:T(8,128)(2,1)S(1)} %bitcast.10), custom_call_target="tpu_custom_call" | custom-call | flops 10000000000 | bytes 10000000 | tf_op jit(solution)/shard_map/forward_pairs/pallas_call | solution.py:583
  28.4 10.4 %combine_rows.1.logs_ref = f32[16,8,128]{2,1,0:T(8,128)S(1)} custom-call(f32[2,8,1536]{2,1,0:T(8,128)S(1)} %get-tuple-element.22.stat), custom_call_target="tpu_custom_call" | custom-call | flops 10000000000 | bytes 10000000 | tf_op jit(solution)/shard_map/combine_rows/pallas_call | solution.py:591
  38.8 6.8 %backward_pairs.1 = (bf16[2,4,4,128,128]{4,3,2,1,0:T(8,128)(2,1)S(1)}, bf16[16,2,128,128]{3,2,1,0:T(8,128)(2,1)S(1)}) custom-call(s32[2,16,128]{2,1,0:T(8,128)S(1)} %get-tuple-element.19.info, bf16[2048,128]{1,0:T(8,128)(2,1)S(1)} %bitcast.13, bf16[2048,128]{1,0:T(8,128)(2,1)S(1)} %bitcast.15, bf16[2048,256]{1,0:T(8,128)(2,1)S(1)} %bitcast.9, ...), custom_call_target="tpu_custom_call" | custom-call | flops 10000000000 | bytes 10000000 | tf_op jit(solution)/shard_map/backward_pairs/pallas_call | solution.py:604
  45.7 41.7 %reduce_gradients.1 = (bf16[64,256]{1,0:T(8,128)(2,1)S(1)}, bf16[64,256]{1,0:T(8,128)(2,1)S(1)}, bf16[64,256]{1,0:T(8,128)(2,1)S(1)}, bf16[64,256]{1,0:T(8,128)(2,1)S(1)}) custom-call(bf16[2,4,4,128,128]{4,3,2,1,0:T(8,128)(2,1)S(1)} %get-tuple-element.24.tiles, bf16[16,2,128,128]{3,2,1,0:T(8,128)(2,1)S(1)} %get-tuple-element.25.dkv), custom_call_target="tpu_custom_call" | custom-call | flops 10000000000 | bytes 10000000 | tf_op jit(solution)/shard_map/reduce_gradients/pallas_call | solution.py:614
  87.4 0.7 leave.1
Async XLA Ops:
  2.7 21.1 %copy-start = (bf16[1,2048,256]{2,1,0:T(8,128)(2,1)S(1)}, bf16[1,2048,256]{2,1,0:T(8,128)(2,1)}, u32[]{:S(2)}) copy-start(bf16[1,2048,256]{2,1,0:T(8,128)(2,1)} %param.7) | copy-start | bytes 3145732
  2.7 21.1 %copy-start.1 = (bf16[1,2048,256]{2,1,0:T(8,128)(2,1)S(1)}, bf16[1,2048,256]{2,1,0:T(8,128)(2,1)}, u32[]{:S(2)}) copy-start(bf16[1,2048,256]{2,1,0:T(8,128)(2,1)} %param.8) | copy-start | bytes 3145732

commit v4 on v3

--- a/solution.py
+++ b/solution.py
@@ -15,7 +15,8 @@
 HALF = D // 2
 HH = H // 2
 NX = 4
-TOGETHER = 4
+TOGETHER = 8
+GROUP = 3
 MESH = pl.DeviceIdType.MESH
 SCALE = 1.0 / math.sqrt(HD)
 LOG2E = math.log2(math.e)
@@ -194,7 +195,7 @@
     return slice(h * BLK, (h + 1) * BLK), slice(h * HD, (h + 1) * HD)
 
 
-def forward_kernel(key_blocks, info, q_ref, g_ref, k_ref, v_ref, acc, stat, vt_ref, qbd, top, tot):
+def forward_kernel(key_blocks, info, q_ref, g_ref, k_ref, v_ref, acc, stat, qbd, vt_ref, top, tot):
     own = half_at(info[0, 2, 0])
     turn_blocks(v_ref, own, vt_ref)
     blocks = qbd.shape[0] - 1
@@ -255,7 +256,7 @@
     return finish
 
 
-def combine_kernel(n, stat, logs, got, middle, sems):
+def combine_kernel(n, stat, g_ref, k_ref, logs, gbd, kt_ref, got, middle, sems):
     row, me = lax.axis_index("row"), lax.axis_index("col")
     y, x = me // NX, lax.rem(me, NX)
     ny = n // NX
@@ -290,6 +291,7 @@
 
     for r in range(2):
         start(0, r, stat.at[r])
+    block_diagonal(((g_ref, gbd),))
     for r in range(2):
         all_of(0, r).wait_recv()
         top, tot, dots = merged(0, r)
@@ -297,6 +299,7 @@
         middle[r, HH:H, :lanes] = tot
         middle[r, :, lanes:] = dots
         start(1, r, middle.at[r])
+    turn_blocks(k_ref, half_at(lax.rem(row, 2)), kt_ref)
     for r in range(2):
         all_of(1, r).wait_recv()
         top, tot, dots = merged(1, r)
@@ -312,13 +315,11 @@
 
 
 def backward_kernel(
-    key_blocks, info, q_ref, g_ref, k_ref, v_ref, logs_ref, weighted, stat,
-    tiles, dkv, kt_ref, qbd, gbd, logs, dq_acc, dk_acc, dv_acc
+    key_blocks, info, qbd, gbd, k_ref, v_ref, kt_ref, logs_ref, weighted, stat,
+    tiles, dkv, logs, dq_acc, dk_acc, dv_acc
 ):
     blocks = qbd.shape[0] - 1
     own = half_at(info[0, 2, 0])
-    turn_blocks(k_ref, own, kt_ref)
-    block_diagonal(((q_ref, qbd), (g_ref, gbd)))
     dq_acc[...] = jnp.zeros_like(dq_acc)
     dk_acc[...] = jnp.zeros_like(dk_acc)
     dv_acc[...] = jnp.zeros_like(dv_acc)
@@ -382,16 +383,17 @@
     lax.fori_loop(0, dkv.shape[0], finish, 0, unroll=4)
 
 
-def chains(n):
-    up, down = n // 2, n - 1 - n // 2
-    near = (up + 1) // 2
-    found = []
-    for first, last in ((near, 1), (up, near + 1)):
-        for sign, far in ((1, up), (-1, down)):
-            senders = list(range(min(first, far), last - 1, -1))
-            if senders:
-                found.append((sign, senders))
-    return found
+def tree(n):
+    steps = []
+    for sign, far in ((1, n // 2), (-1, n - 1 - n // 2)):
+        depth = {}
+        for o in range(far, 0, -1):
+            to = max(o - GROUP, 0) if o % GROUP == 0 else o - 1
+            depth[to] = max(depth.get(to, 0), depth.get(o, 0) + 1)
+            steps.append((depth.get(o, 0), sign, o, to))
+    return [
+        [step[1:] for step in steps if step[0] == level] for level in range(max(s[0] for s in steps) + 1)
+    ]
 
 
 def reduce_kernel(
@@ -403,10 +405,10 @@
     ny = n_col // NX
     sibling = (row + 1 - 2 * h, me)
     xs, ys = others(x, NX), others(y, ny)
-    ring = chains(n_z)
-    hops = [
-        [sign * (o - after) for o, after in zip(senders, senders[1:] + [0])] for sign, senders in ring
-    ]
+    levels = tree(n_z)
+    edges = [edge for level in levels for edge in level]
+    ends = [edge for edge in edges if edge[2] == 0]
+    inner = [edge for edge in edges if edge[2] != 0]
 
     def at_z(delta, core):
         return (lax.rem(z + n_z + delta, n_z) * 2 + core, me)
@@ -419,46 +421,45 @@
 
     meet(
         [sibling]
-        + [at_z(d, h) for d in both_ways([d for c in hops for d in c])]
-        + [at_z(d, 1 - h) for d in both_ways([c[-1] for c in hops])]
+        + [at_z(d, h) for d in both_ways([sign * (o - to) for sign, o, to in edges])]
+        + [at_z(d, 1 - h) for d in both_ways([sign * o for sign, o, _ in ends])]
         + [(row, y * NX + p) for p in xs]
         + [(row, p * NX + x) for p in ys]
     )
-    slots = {}
-
-    def arrived(i, c, s):
-        slot = slots[c, s]
+
+    def arrived(i, slot):
         ref = come.at[i, slot]
         remote(ref, ref, send_sem, come_sems.at[i, slot], sibling).wait_recv()
         return come[i, slot]
 
-    def pass_on(s):
-        for i in range(2):
-            for c, (sign, senders) in enumerate(ring):
-                if s >= len(senders):
-                    continue
-                target = lax.rem(z + n_z + sign * senders[s], n_z)
-                if s == len(senders) - 1:
-                    sent[i, c] = dkv[target, i] + arrived(i, c, s - 1) if s else dkv[target, i]
-                    if i == 1:
-                        for core in range(2):
-                            remote(
-                                sent.at[:, c, core * (BLK // 2) : (core + 1) * (BLK // 2)],
-                                ended.at[c, h],
-                                end_send,
-                                end_sems.at[c, h],
-                                at_z(hops[c][s], core),
-                            ).start()
-                    continue
-                slot = slots.setdefault((c, s), len(slots))
-                if s == 0:
-                    src = dkv.at[target, i]
-                else:
-                    src = sent.at[i, len(ring) + slot]
-                    sent[i, len(ring) + slot] = dkv[target, i] + arrived(i, c, s - 1)
-                remote(
-                    src, come.at[i, slot], send_sem, come_sems.at[i, slot], at_z(hops[c][s], h)
-                ).start()
+    def pass_on(level):
+        for edge in sorted(level, key=lambda e: -e[1]):
+            for i in range(2):
+                sign, o, to = edge
+                target = lax.rem(z + n_z + sign * o, n_z)
+                src = dkv.at[target, i]
+                from_slots = [k for k, e in enumerate(inner) if (e[0], e[2]) == (sign, o)]
+                if from_slots or edge in ends:
+                    value = dkv[target, i]
+                    for k in from_slots:
+                        value = value + arrived(i, k)
+                    src = sent.at[i, edges.index(edge)]
+                    src[...] = value
+                if edge in inner:
+                    slot = inner.index(edge)
+                    remote(
+                        src, come.at[i, slot], send_sem, come_sems.at[i, slot], at_z(sign * (o - to), h)
+                    ).start()
+                elif i == 1:
+                    slot = ends.index(edge)
+                    for core in range(2):
+                        remote(
+                            sent.at[:, edges.index(edge), core * (BLK // 2) : (core + 1) * (BLK // 2)],
+                            ended.at[slot, h],
+                            end_send,
+                            end_sems.at[slot, h],
+                            at_z(sign * o, core),
+                        ).start()
 
     along_x = (x, NX, [(p, (row, y * NX + p)) for p in xs])
     along_y = (y, ny, [(p, (row, p * NX + x)) for p in ys])
@@ -484,16 +485,15 @@
         refs = [first[i, k, at] if step == 0 else last[i, k] for k in range(size)]
         return functools.reduce(jnp.add, [ref.astype(jnp.float32) for ref in refs])
 
-    pass_on(0)
+    pass_on(levels[0])
     aside = remote(dkv.at[z, :, lanes_of(1 - h)], beside, beside_sems.at[0], beside_sems.at[1], sibling)
     aside.start()
     for i in range(2):
         spread(i, 0)
-    most = max(len(senders) for _, senders in ring)
     finishes = []
-    for s in range(1, max(most, 4)):
-        if s < most:
-            pass_on(s)
+    for s in range(1, max(len(levels), 4)):
+        if s < len(levels):
+            pass_on(levels[s])
         for i in range(2):
             if s == 2:
                 phase(i, 0).wait_recv()
@@ -510,7 +510,7 @@
     for finish in finishes:
         finish()
     totals = [dkv[z, :, lanes_of(h)].astype(jnp.float32), beside[...].astype(jnp.float32)]
-    for c in range(len(ring)):
+    for c in range(len(ends)):
         for k, core in enumerate((h, 1 - h)):
             ref = ended.at[c, core]
             remote(ref, ref, end_send, end_sems.at[c, core], sibling).wait_recv()
@@ -533,23 +533,19 @@
 
 
 def fwd_scratch(blocks, lanes):
-    bf16, f32 = jnp.bfloat16, jnp.float32
+    f32 = jnp.float32
     rows = blocks * BLK
     return [
-        pltpu.VMEM((HALF, lanes), bf16),
-        pltpu.VMEM((blocks + 1, HH * BLK, HALF), bf16),
+        pltpu.VMEM((HALF, lanes), jnp.bfloat16),
         pltpu.VMEM((HH, rows + BLK), f32),
         pltpu.VMEM((HH, rows + BLK), f32),
     ]
 
 
 def bwd_scratch(blocks, lanes):
-    bf16, f32 = jnp.bfloat16, jnp.float32
+    f32 = jnp.float32
     rows = blocks * BLK
     return [
-        pltpu.VMEM((HALF, lanes), bf16),
-        pltpu.VMEM((blocks + 1, HH * BLK, HALF), bf16),
-        pltpu.VMEM((blocks + 1, HH * BLK, HALF), bf16),
         pltpu.VMEM((blocks + 1, H, BLK), f32),
         pltpu.VMEM((HALF, rows + BLK), f32),
         pltpu.VMEM((lanes, HALF), f32),
@@ -580,37 +576,39 @@
     all_q, all_g = all_q.reshape(rows, HALF), all_g.reshape(rows, HALF)
 
     folded = (H, rows // 2 * 3 // 2)
-    weighted, stat = call(
+    by_head = shape((blocks + 1, HH * BLK, HALF), bf16)
+    weighted, stat, qbd = call(
         functools.partial(forward_kernel, key_blocks),
         "forward_pairs",
-        (shape((HALF, rows + BLK), f32), shape((2, *folded), f32)),
+        (shape((HALF, rows + BLK), f32), shape((2, *folded), f32), by_head),
         [smem] + [vmem] * 4,
         fwd_scratch(blocks, lanes),
     )(info, all_q, all_g, keys, vals)
 
-    logs = call(
+    logs, gbd, keys_t = call(
         functools.partial(combine_kernel, n_col),
         "combine_rows",
-        shape((blocks, H, BLK), f32),
-        [vmem],
+        (shape((blocks, H, BLK), f32), by_head, shape((HALF, lanes), bf16)),
+        [vmem] * 3,
         [
             pltpu.VMEM((2, 2, max(NX, ny), *folded), f32),
             pltpu.VMEM((2, *folded), f32),
             dma((2, 2, 2)),
         ],
         1,
-    )(stat)
+    )(stat, all_g, keys)
 
     tiles, dkv = call(
         functools.partial(backward_kernel, key_blocks),
         "backward_pairs",
         (shape((2, ny, NX, HALF, BLK), bf16), shape((key_blocks, 2, BLK, HALF), bf16)),
-        [smem] + [vmem] * 7,
+        [smem] + [vmem] * 8,
         bwd_scratch(blocks, lanes),
-    )(info, all_q, all_g, keys, vals, logs, weighted, stat)
+    )(info, qbd, gbd, keys, vals, keys_t, logs, weighted, stat)
 
     side = max(NX, ny)
-    n_chains, n_sent = len(chains(n_z)), sum(len(senders) for _, senders in chains(n_z))
+    edges = [edge for level in tree(n_z) for edge in level]
+    n_sent, n_ends = len(edges), sum(edge[2] == 0 for edge in edges)
     grads = call(
         functools.partial(reduce_kernel, n_col, n_z),
         "reduce_gradients",
@@ -623,15 +621,15 @@
             pltpu.VMEM((2, BLK, HALF), bf16),
             pltpu.VMEM((2, own_rows, HALF), bf16),
             pltpu.VMEM((2, n_sent, BLK, HALF), bf16),
-            pltpu.VMEM((2, n_sent - n_chains, BLK, HALF), bf16),
-            pltpu.VMEM((n_chains, 2, 2, own_rows, HALF), bf16),
+            pltpu.VMEM((2, n_sent - n_ends, BLK, HALF), bf16),
+            pltpu.VMEM((n_ends, 2, 2, own_rows, HALF), bf16),
             pltpu.VMEM((2, own_rows, HALF), bf16),
             dma((2, 2, 2)),
             dma((2, 2)),
             dma,
-            dma((2, n_sent - n_chains)),
+            dma((2, n_sent - n_ends)),
             dma,
-            dma((n_chains, 2)),
+            dma((n_ends, 2)),
             dma((2,)),
         ],
         2,

time: 88.3 us -> 83.1 us (0.941)
  Pallas kernels: 85.2 us -> 80 us
    pallas_call x1, Pallas kernels: 41.7 us -> 37.2 us  [shards(): call(functools.partial(reduce_kernel, n_col, n_z), 'reduce_gradients', (s...]
where the time goes in v4:
time: 83.1 us; the launch traced here: 82.9 us
  Pallas kernels  80 us (96%)
  other arithmetic  1.44 us (2%)
  between operations  1.36 us (2%)
    pallas_call x1, Pallas kernels, shards(): call(functools.partial(reduce_kernel, n_col, n_z), 'reduce_gradients', (s...  37.2 us
    pallas_call x1, Pallas kernels, shards(): call(functools.partial(gather_kernel, n_col), 'gather_lanes', (shape((2,...  21 us
    pallas_call x1, Pallas kernels, shards(): call(functools.partial(combine_kernel, n_col), 'combine_rows', (shape((bl...  10.4 us
    pallas_call x1, Pallas kernels, shards(): call(functools.partial(backward_kernel, key_blocks), 'backward_pairs', (s...  6.43 us
    pallas_call x1, Pallas kernels, shards(): call(functools.partial(forward_kernel, key_blocks), 'forward_pairs', (sha...  4.26 us

profile of v4, /device:TPU:1, one launch (start us, length us, event | category | flops | bytes accessed | tf_op | source)
XLA Modules:
  0.0 82.9 jit_solution(6786417005341636932)
XLA Ops:
  1.3 0.7 convert_bitcast_fusion
  1.9 0.8 fusion.4.own_ref
  2.7 0.0 copy-start
  2.7 0.0 copy-start.1
  2.8 21.0 %gather_lanes.1 = (bf16[2,4,4,64,128]{4,3,2,1,0:T(8,128)(2,1)S(1)}, bf16[2,4,4,64,128]{4,3,2,1,0:T(8,128)(2,1)S(1)}, s32[2,16,128]{2,1,0:T(8,128)S(1)}) custom-call(bf16[144,256]{1,0:T(8,128)(2,1)S(1)} %fusion.4.own_ref), custom_call_target="tpu_custom_call" | custom-call | flops 10000000000 | bytes 10000000 | tf_op jit(solution)/shard_map/gather_lanes/pallas_call | solution.py:568
  23.8 0.0 copy-done
  23.8 0.0 copy-done.1
  23.8 4.3 %forward_pairs.1 = (f32[128,2176]{1,0:T(8,128)S(1)}, f32[2,8,1536]{2,1,0:T(8,128)S(1)}, bf16[17,512,128]{2,1,0:T(8,128)(2,1)S(1)}) custom-call(s32[2,16,128]{2,1,0:T(8,128)S(1)} %get-tuple-element.23.info, bf16[2048,128]{1,0:T(8,128)(2,1)S(1)} %bitcast.15, bf16[2048,128]{1,0:T(8,128)(2,1)S(1)} %bitcast.13, bf16[2048,256]{1,0:T(8,128)(2,1)S(1)} %bitcast.8, ...), custom_call_target="tpu_custom_call" | custom-call | flops 10000000000 | bytes 10000000 | tf_op jit(solution)/shard_map/forward_pairs/pallas_call | solution.py:580
  28.1 10.4 %combine_rows.1 = (f32[16,8,128]{2,1,0:T(8,128)S(1)}, bf16[17,512,128]{2,1,0:T(8,128)(2,1)S(1)}, bf16[128,2048]{1,0:T(8,128)(2,1)S(1)}) custom-call(f32[2,8,1536]{2,1,0:T(8,128)S(1)} %get-tuple-element.27.stat, bf16[2048,128]{1,0:T(8,128)(2,1)S(1)} %bitcast.14, bf16[2048,256]{1,0:T(8,128)(2,1)S(1)} %bitcast.9), custom_call_target="tpu_custom_call" | custom-call | flops 10000000000 | bytes 10000000 | tf_op jit(solution)/shard_map/combine_rows/pallas_call | solution.py:588
  38.5 6.4 %backward_pairs.1 = (bf16[2,4,4,128,128]{4,3,2,1,0:T(8,128)(2,1)S(1)}, bf16[16,2,128,128]{3,2,1,0:T(8,128)(2,1)S(1)}) custom-call(s32[2,16,128]{2,1,0:T(8,128)S(1)} %get-tuple-element.23.info, bf16[17,512,128]{2,1,0:T(8,128)(2,1)S(1)} %get-tuple-element.26.qbd, bf16[17,512,128]{2,1,0:T(8,128)(2,1)S(1)} %get-tuple-element.28.gbd, ...), custom_call_target="tpu_custom_call" | custom-call | flops 10000000000 | bytes 10000000 | tf_op jit(solution)/shard_map/backward_pairs/pallas_call | solution.py:601
  45.0 37.2 %reduce_gradients.1 = (bf16[64,256]{1,0:T(8,128)(2,1)S(1)}, bf16[64,256]{1,0:T(8,128)(2,1)S(1)}, bf16[64,256]{1,0:T(8,128)(2,1)S(1)}, bf16[64,256]{1,0:T(8,128)(2,1)S(1)}) custom-call(bf16[2,4,4,128,128]{4,3,2,1,0:T(8,128)(2,1)S(1)} %get-tuple-element.32.tiles, bf16[16,2,128,128]{3,2,1,0:T(8,128)(2,1)S(1)} %get-tuple-element.33.dkv), custom_call_target="tpu_custom_call" | custom-call | flops 10000000000 | bytes 10000000 | tf_op jit(solution)/shard_map/reduce_gradients/pallas_call | solution.py:612
  82.2 0.7 leave.1
Async XLA Ops:
  2.7 21.1 %copy-start = (bf16[1,2048,256]{2,1,0:T(8,128)(2,1)S(1)}, bf16[1,2048,256]{2,1,0:T(8,128)(2,1)}, u32[]{:S(2)}) copy-start(bf16[1,2048,256]{2,1,0:T(8,128)(2,1)} %param.7) | copy-start | bytes 3145732
  2.7 21.1 %copy-start.1 = (bf16[1,2048,256]{2,1,0:T(8,128)(2,1)S(1)}, bf16[1,2048,256]{2,1,0:T(8,128)(2,1)}, u32[]{:S(2)}) copy-start(bf16[1,2048,256]{2,1,0:T(8,128)(2,1)} %param.8) | copy-start | bytes 3145732

commit v5 on v4

--- a/solution.py
+++ b/solution.py
@@ -389,8 +389,9 @@
         depth = {}
         for o in range(far, 0, -1):
             to = max(o - GROUP, 0) if o % GROUP == 0 else o - 1
-            depth[to] = max(depth.get(to, 0), depth.get(o, 0) + 1)
-            steps.append((depth.get(o, 0), sign, o, to))
+            level = max(depth.get(o, 0), 2 if o - to > 1 else 0)
+            depth[to] = max(depth.get(to, 0), level + 1)
+            steps.append((level, sign, o, to))
     return [
         [step[1:] for step in steps if step[0] == level] for level in range(max(s[0] for s in steps) + 1)
     ]
@@ -413,29 +414,34 @@
     def at_z(delta, core):
         return (lax.rem(z + n_z + delta, n_z) * 2 + core, me)
 
-    def both_ways(deltas):
-        return sorted({d % n_z for d in deltas} | {-d % n_z for d in deltas})
-
     def lanes_of(core):
         return pl.ds(pl.multiple_of(core * (BLK // 2), BLK // 2), BLK // 2)
 
     meet(
         [sibling]
-        + [at_z(d, h) for d in both_ways([sign * (o - to) for sign, o, to in edges])]
-        + [at_z(d, 1 - h) for d in both_ways([sign * o for sign, o, _ in ends])]
+        + [at_z(d, core) for d in sorted({1, n_z - 1}) for core in (h, 1 - h)]
         + [(row, y * NX + p) for p in xs]
         + [(row, p * NX + x) for p in ys]
     )
 
+    seen = set()
+
     def arrived(i, slot):
-        ref = come.at[i, slot]
-        remote(ref, ref, send_sem, come_sems.at[i, slot], sibling).wait_recv()
+        if (i, slot) not in seen:
+            ref = come.at[i, slot]
+            remote(ref, ref, send_sem, come_sems.at[i, slot], sibling).wait_recv()
+            seen.add((i, slot))
         return come[i, slot]
+
+    relayed = [inner.index((sign, GROUP + 1, GROUP)) for sign in (1, -1)]
 
     def pass_on(level):
         for edge in sorted(level, key=lambda e: -e[1]):
             for i in range(2):
                 sign, o, to = edge
+                if o - to > 1:
+                    for slot in relayed:
+                        arrived(0, slot)
                 target = lax.rem(z + n_z + sign * o, n_z)
                 src = dkv.at[target, i]
                 from_slots = [k for k, e in enumerate(inner) if (e[0], e[2]) == (sign, o)]

time: 83.1 us -> 83.6 us (level)
    pallas_call x1, Pallas kernels: 37.2 us -> 32.8 us  [shards(): call(functools.partial(reduce_kernel, n_col, n_z), 'reduce_gradients', (s...]
    pallas_call x1, Pallas kernels: 6.43 us -> 9.71 us  [shards(): call(functools.partial(backward_kernel, key_blocks), 'backward_pairs', (s...]
    pallas_call x1, Pallas kernels: 4.26 us -> 5.92 us  [shards(): call(functools.partial(forward_kernel, key_blocks), 'forward_pairs', (sha...]
where the time goes in v5:
time: 83.6 us; the launch traced here: 83.4 us
  Pallas kernels  80.5 us (96%)
  other arithmetic  1.44 us (2%)
  between operations  1.36 us (2%)
    pallas_call x1, Pallas kernels, shards(): call(functools.partial(reduce_kernel, n_col, n_z), 'reduce_gradients', (s...  32.8 us
    pallas_call x1, Pallas kernels, shards(): call(functools.partial(gather_kernel, n_col), 'gather_lanes', (shape((2,...  21 us
    pallas_call x1, Pallas kernels, shards(): call(functools.partial(combine_kernel, n_col), 'combine_rows', (shape((bl...  10.4 us
    pallas_call x1, Pallas kernels, shards(): call(functools.partial(backward_kernel, key_blocks), 'backward_pairs', (s...  9.71 us
    pallas_call x1, Pallas kernels, shards(): call(functools.partial(forward_kernel, key_blocks), 'forward_pairs', (sha...  5.92 us

profile of v5, /device:TPU:1, one launch (start us, length us, event | category | flops | bytes accessed | tf_op | source)
XLA Modules:
  0.0 83.4 jit_solution(1021839381834900893)
XLA Ops:
  1.3 0.7 convert_bitcast_fusion
  1.9 0.8 fusion.4.own_ref
  2.7 0.0 copy-start
  2.7 0.0 copy-start.1
  2.8 21.0 %gather_lanes.1 = (bf16[2,4,4,64,128]{4,3,2,1,0:T(8,128)(2,1)S(1)}, bf16[2,4,4,64,128]{4,3,2,1,0:T(8,128)(2,1)S(1)}, s32[2,16,128]{2,1,0:T(8,128)S(1)}) custom-call(bf16[144,256]{1,0:T(8,128)(2,1)S(1)} %fusion.4.own_ref), custom_call_target="tpu_custom_call" | custom-call | flops 10000000000 | bytes 10000000 | tf_op jit(solution)/shard_map/gather_lanes/pallas_call | solution.py:574
  23.8 0.0 copy-done
  23.8 0.0 copy-done.1
  23.8 5.9 %forward_pairs.1 = (f32[128,2176]{1,0:T(8,128)S(1)}, f32[2,8,1536]{2,1,0:T(8,128)S(1)}, bf16[17,512,128]{2,1,0:T(8,128)(2,1)S(1)}) custom-call(s32[2,16,128]{2,1,0:T(8,128)S(1)} %get-tuple-element.23.info, bf16[2048,128]{1,0:T(8,128)(2,1)S(1)} %bitcast.15, bf16[2048,128]{1,0:T(8,128)(2,1)S(1)} %bitcast.13, bf16[2048,256]{1,0:T(8,128)(2,1)S(1)} %bitcast.8, ...), custom_call_target="tpu_custom_call" | custom-call | flops 10000000000 | bytes 10000000 | tf_op jit(solution)/shard_map/forward_pairs/pallas_call | solution.py:586
  29.8 10.4 %combine_rows.1 = (f32[16,8,128]{2,1,0:T(8,128)S(1)}, bf16[17,512,128]{2,1,0:T(8,128)(2,1)S(1)}, bf16[128,2048]{1,0:T(8,128)(2,1)S(1)}) custom-call(f32[2,8,1536]{2,1,0:T(8,128)S(1)} %get-tuple-element.27.stat, bf16[2048,128]{1,0:T(8,128)(2,1)S(1)} %bitcast.14, bf16[2048,256]{1,0:T(8,128)(2,1)S(1)} %bitcast.9), custom_call_target="tpu_custom_call" | custom-call | flops 10000000000 | bytes 10000000 | tf_op jit(solution)/shard_map/combine_rows/pallas_call | solution.py:594
  40.2 9.7 %backward_pairs.1 = (bf16[2,4,4,128,128]{4,3,2,1,0:T(8,128)(2,1)S(1)}, bf16[16,2,128,128]{3,2,1,0:T(8,128)(2,1)S(1)}) custom-call(s32[2,16,128]{2,1,0:T(8,128)S(1)} %get-tuple-element.23.info, bf16[17,512,128]{2,1,0:T(8,128)(2,1)S(1)} %get-tuple-element.26.qbd, bf16[17,512,128]{2,1,0:T(8,128)(2,1)S(1)} %get-tuple-element.28.gbd, ...), custom_call_target="tpu_custom_call" | custom-call | flops 10000000000 | bytes 10000000 | tf_op jit(solution)/shard_map/backward_pairs/pallas_call | solution.py:607
  49.9 32.8 %reduce_gradients.1 = (bf16[64,256]{1,0:T(8,128)(2,1)S(1)}, bf16[64,256]{1,0:T(8,128)(2,1)S(1)}, bf16[64,256]{1,0:T(8,128)(2,1)S(1)}, bf16[64,256]{1,0:T(8,128)(2,1)S(1)}) custom-call(bf16[2,4,4,128,128]{4,3,2,1,0:T(8,128)(2,1)S(1)} %get-tuple-element.32.tiles, bf16[16,2,128,128]{3,2,1,0:T(8,128)(2,1)S(1)} %get-tuple-element.33.dkv), custom_call_target="tpu_custom_call" | custom-call | flops 10000000000 | bytes 10000000 | tf_op jit(solution)/shard_map/reduce_gradients/pallas_call | solution.py:618
  82.7 0.7 leave.1
Async XLA Ops:
  2.7 21.1 %copy-start = (bf16[1,2048,256]{2,1,0:T(8,128)(2,1)S(1)}, bf16[1,2048,256]{2,1,0:T(8,128)(2,1)}, u32[]{:S(2)}) copy-start(bf16[1,2048,256]{2,1,0:T(8,128)(2,1)} %param.7) | copy-start | bytes 3145732
  2.7 21.1 %copy-start.1 = (bf16[1,2048,256]{2,1,0:T(8,128)(2,1)S(1)}, bf16[1,2048,256]{2,1,0:T(8,128)(2,1)}, u32[]{:S(2)}) copy-start(bf16[1,2048,256]{2,1,0:T(8,128)(2,1)} %param.8) | copy-start | bytes 3145732

commit v6 on v5

--- a/solution.py
+++ b/solution.py
@@ -69,6 +69,10 @@
     return [lax.rem(me + k, n) for k in range(1, n)]
 
 
+def farthest(me, n):
+    return [lax.rem(me + k, n) for k in sorted(range(1, n), key=lambda k: -min(k, n - k))]
+
+
 def block_diagonal(pairs):
     blocks = pairs[0][1].shape[0] - 1
     lane = lax.broadcasted_iota(jnp.int32, (BLK, HALF), 1)
@@ -123,8 +127,8 @@
     ny = n_col // NX
     rows = qo.shape[3]
     sibling = (row + 1 - 2 * h, me)
-    along_x = [(row, y * NX + p) for p in others(x, NX)]
-    along_y = [(row, p * NX + x) for p in others(y, ny)]
+    along_x = [(row, y * NX + p) for p in farthest(x, NX)]
+    along_y = [(row, p * NX + x) for p in farthest(y, ny)]
     meet([sibling] + along_x + along_y)
     swaps = [
         remote(src, dst, swap_sems.at[0, i], swap_sems.at[1, i], sibling)
@@ -261,8 +265,8 @@
     y, x = me // NX, lax.rem(me, NX)
     ny = n // NX
     lanes = stat.shape[2] * 2 // 3
-    along_x = (x, NX, [(row, y * NX + p) for p in others(x, NX)])
-    along_y = (y, ny, [(row, p * NX + x) for p in others(y, ny)])
+    along_x = (x, NX, [(row, y * NX + p) for p in farthest(x, NX)])
+    along_y = (y, ny, [(row, p * NX + x) for p in farthest(y, ny)])
     meet(along_x[2] + along_y[2])
 
     def start(phase, r, src):
@@ -315,8 +319,7 @@
 
 
 def backward_kernel(
-    key_blocks, info, qbd, gbd, k_ref, v_ref, kt_ref, logs_ref, weighted, stat,
-    tiles, dkv, logs, dq_acc, dk_acc, dv_acc
+    key_blocks, info, qbd, gbd, k_ref, v_ref, kt_ref, logs_ref, dq_acc, dkv, logs, dk_acc, dv_acc
 ):
     blocks = qbd.shape[0] - 1
     own = half_at(info[0, 2, 0])
@@ -360,6 +363,17 @@
                 dq_acc[head(h)[1], q_at] += qs[h]
 
     each_pair(info, key_blocks, blocks // 2, TOGETHER, visit)
+    def finish(b, carry):
+        at = pl.ds(pl.multiple_of(b * BLK, BLK), BLK)
+        dkv[b, 0] = (dk_acc[at, :] * SCALE).astype(jnp.bfloat16)
+        dkv[b, 1] = dv_acc[at, :].astype(jnp.bfloat16)
+        return carry
+
+    lax.fori_loop(0, dkv.shape[0], finish, 0, unroll=4)
+
+
+def make_tiles(dq_acc, weighted, stat, logs, tiles):
+    blocks = logs.shape[0]
     for b in range(blocks // 2):
         at = slice(b * BLK, (b + 1) * BLK)
         grads, normed = [], []
@@ -374,14 +388,6 @@
             for k, tile in enumerate(interleave(*both)):
                 tiles[i, (2 * b + k) // NX, (2 * b + k) % NX] = tile.astype(jnp.bfloat16)
 
-    def finish(b, carry):
-        at = pl.ds(pl.multiple_of(b * BLK, BLK), BLK)
-        dkv[b, 0] = (dk_acc[at, :] * SCALE).astype(jnp.bfloat16)
-        dkv[b, 1] = dv_acc[at, :].astype(jnp.bfloat16)
-        return carry
-
-    lax.fori_loop(0, dkv.shape[0], finish, 0, unroll=4)
-
 
 def tree(n):
     steps = []
@@ -392,13 +398,14 @@
             level = max(depth.get(o, 0), 2 if o - to > 1 else 0)
             depth[to] = max(depth.get(to, 0), level + 1)
             steps.append((level, sign, o, to))
+    last = max(step[0] for step in steps)
     return [
-        [step[1:] for step in steps if step[0] == level] for level in range(max(s[0] for s in steps) + 1)
+        [step[1:] for step in steps if level == (step[0] if step[3] else last)] for level in range(last + 1)
     ]
 
 
 def reduce_kernel(
-    n_col, n_z, tiles, dkv, out_q, out_k, out_v, out_a, first, middle, last, mine, got, sent, come, ended, beside,
+    n_col, n_z, dq_acc, dkv, weighted, stat, logs, out_q, out_k, out_v, out_a, tiles, first, middle, last, mine, got, sent, come, ended, beside,
     phase_sems, swap_sems, send_sem, come_sems, end_send, end_sems, beside_sems
 ):
     row, me = lax.axis_index("row"), lax.axis_index("col")
@@ -417,12 +424,10 @@
     def lanes_of(core):
         return pl.ds(pl.multiple_of(core * (BLK // 2), BLK // 2), BLK // 2)
 
-    meet(
-        [sibling]
-        + [at_z(d, core) for d in sorted({1, n_z - 1}) for core in (h, 1 - h)]
-        + [(row, y * NX + p) for p in xs]
-        + [(row, p * NX + x) for p in ys]
-    )
+    along_x = (x, NX, [(row, y * NX + p) for p in xs])
+    along_y = (y, ny, [(row, p * NX + x) for p in ys])
+    near = [line[2][k] for line in (along_x, along_y) for k in (0, -1)]
+    meet([sibling, at_z(1, h), at_z(-1, h)] + near)
 
     seen = set()
 
@@ -467,23 +472,25 @@
                             at_z(sign * o, core),
                         ).start()
 
-    along_x = (x, NX, [(p, (row, y * NX + p)) for p in xs])
-    along_y = (y, ny, [(p, (row, p * NX + x)) for p in ys])
-
-    def phase(i, step):
-        size = (along_x, along_y)[i ^ step][1]
-        ref = (first, last)[step].at[i, 0 : size - 1]
-        return remote(ref, ref, phase_sems.at[0, i, step], phase_sems.at[1, i, step], sibling)
-
-    def spread(i, step):
-        here, size, peers = (along_x, along_y)[i ^ step]
-        for p, device in peers:
+    def phase(i, step, part):
+        size = (along_x, along_y)[i ^ step][1] - 1
+        count = size if step else (2, size - 2)[part]
+        ref = (first, last)[step].at[i, 0:count]
+        return remote(ref, ref, phase_sems.at[0, i, step, part], phase_sems.at[1, i, step, part], sibling)
+
+    def spread(i, step, part):
+        here, _, peers = (along_x, along_y)[i ^ step]
+        chosen = peers if step else (peers[:1] + peers[-1:], peers[1:-1])[part]
+        for device in chosen:
+            p = device[1] // NX if (i ^ step) else lax.rem(device[1], NX)
             src = middle.at[i, p] if step else (tiles.at[0, :, p] if i == 0 else tiles.at[1, p])
             dst = (first, last)[step].at[i, here]
-            remote(src, dst, phase_sems.at[0, i, step], phase_sems.at[1, i, step], device).start()
+            remote(
+                src, dst, phase_sems.at[0, i, step, part], phase_sems.at[1, i, step, part], device
+            ).start()
         if step:
             last[i, here] = middle[i, here]
-        else:
+        elif part == 0:
             first[i, here] = tiles[0, :, x] if i == 0 else tiles[1, y]
 
     def summed(i, step, at):
@@ -491,28 +498,30 @@
         refs = [first[i, k, at] if step == 0 else last[i, k] for k in range(size)]
         return functools.reduce(jnp.add, [ref.astype(jnp.float32) for ref in refs])
 
-    pass_on(levels[0])
     aside = remote(dkv.at[z, :, lanes_of(1 - h)], beside, beside_sems.at[0], beside_sems.at[1], sibling)
-    aside.start()
-    for i in range(2):
-        spread(i, 0)
     finishes = []
-    for s in range(1, max(len(levels), 4)):
-        if s < len(levels):
-            pass_on(levels[s])
+    for s, level in enumerate(levels):
+        if s == len(levels) - 1:
+            aside.start()
+            aside.wait_recv()
+        pass_on(level)
+        if s == 0:
+            make_tiles(dq_acc, weighted, stat, logs, tiles)
+        for i in range(2):
+            if s == 0:
+                spread(i, 0, 0)
+            if s == 1:
+                phase(i, 0, 0).wait_recv()
+                spread(i, 0, 1)
         for i in range(2):
             if s == 2:
-                phase(i, 0).wait_recv()
+                phase(i, 0, 1).wait_recv()
                 for b in range((along_y, along_x)[i][1]):
                     middle[i, b] = summed(i, 0, b).astype(jnp.bfloat16)
-                spread(i, 1)
-            if s == 3:
-                phase(i, 1).wait_recv()
-                out = (out_q, out_a)[i]
-                finishes.append(
-                    swap_rows(summed(i, 1, 0).T, out, mine.at[i], got.at[i], swap_sems.at[i], h, sibling)
-                )
-    aside.wait_recv()
+                spread(i, 1, 0)
+    for i, out in enumerate((out_q, out_a)):
+        phase(i, 1, 0).wait_recv()
+        finishes.append(swap_rows(summed(i, 1, 0).T, out, mine.at[i], got.at[i], swap_sems.at[i], h, sibling))
     for finish in finishes:
         finish()
     totals = [dkv[z, :, lanes_of(h)].astype(jnp.float32), beside[...].astype(jnp.float32)]
@@ -528,8 +537,9 @@
     remote(come, come, send_sem, come_sems.at[0, 0], sibling).wait_send()
     remote(ended, ended, end_send, end_sems.at[0, 0], sibling).wait_send()
     for i in range(2):
-        for step in range(2):
-            phase(i, step).wait_send()
+        phase(i, 0, 0).wait_send()
+        phase(i, 0, 1).wait_send()
+        phase(i, 1, 0).wait_send()
 
 
 def leave_kernel(*refs):
@@ -550,10 +560,8 @@
 
 def bwd_scratch(blocks, lanes):
     f32 = jnp.float32
-    rows = blocks * BLK
     return [
         pltpu.VMEM((blocks + 1, H, BLK), f32),
-        pltpu.VMEM((HALF, rows + BLK), f32),
         pltpu.VMEM((lanes, HALF), f32),
         pltpu.VMEM((lanes, HALF), f32),
     ]
@@ -604,13 +612,13 @@
         1,
     )(stat, all_g, keys)
 
-    tiles, dkv = call(
+    dq, dkv = call(
         functools.partial(backward_kernel, key_blocks),
         "backward_pairs",
-        (shape((2, ny, NX, HALF, BLK), bf16), shape((key_blocks, 2, BLK, HALF), bf16)),
-        [smem] + [vmem] * 8,
+        (shape((HALF, rows + BLK), f32), shape((key_blocks, 2, BLK, HALF), bf16)),
+        [smem] + [vmem] * 6,
         bwd_scratch(blocks, lanes),
-    )(info, qbd, gbd, keys, vals, keys_t, logs, weighted, stat)
+    )(info, qbd, gbd, keys, vals, keys_t, logs)
 
     side = max(NX, ny)
     edges = [edge for level in tree(n_z) for edge in level]
@@ -619,8 +627,9 @@
         functools.partial(reduce_kernel, n_col, n_z),
         "reduce_gradients",
         (shape((own_rows, D), bf16),) * 4,
-        [vmem] * 2,
+        [vmem] * 5,
         [
+            pltpu.VMEM((2, ny, NX, HALF, BLK), bf16),
             pltpu.VMEM((2, side, side, HALF, BLK), bf16),
             pltpu.VMEM((2, side, HALF, BLK), bf16),
             pltpu.VMEM((2, side, HALF, BLK), bf16),
@@ -630,7 +639,7 @@
             pltpu.VMEM((2, n_sent - n_ends, BLK, HALF), bf16),
             pltpu.VMEM((n_ends, 2, 2, own_rows, HALF), bf16),
             pltpu.VMEM((2, own_rows, HALF), bf16),
-            dma((2, 2, 2)),
+            dma((2, 2, 2, 2)),
             dma((2, 2)),
             dma,
             dma((2, n_sent - n_ends)),
@@ -639,7 +648,7 @@
             dma((2,)),
         ],
         2,
-    )(tiles, dkv)
+    )(dq, dkv, weighted, stat, logs)
     grad_q, grad_k, grad_v, attended = call(
         leave_kernel, "leave", (shape((1, own_rows, D), bf16),) * 4, [vmem] * 4, []
     )(*grads)

time: 83.6 us -> 80 us (0.957)
  Pallas kernels: 80.5 us -> 76.5 us
    pallas_call x1, Pallas kernels: 9.71 us -> 6.03 us  [shards(): call(functools.partial(backward_kernel, key_blocks), 'backward_pairs', (s...]
    pallas_call x1, Pallas kernels: 5.92 us -> 4.25 us  [shards(): call(functools.partial(forward_kernel, key_blocks), 'forward_pairs', (sha...]
    pallas_call x1, Pallas kernels: 32.8 us -> 33.9 us  [shards(): call(functools.partial(reduce_kernel, n_col, n_z), 'reduce_gradients', (s...]
where the time goes in v6:
time: 80 us; the launch traced here: 79.3 us
  Pallas kernels  76.5 us (96%)
  other arithmetic  1.44 us (2%)
  between operations  1.36 us (2%)
    pallas_call x1, Pallas kernels, shards(): call(functools.partial(reduce_kernel, n_col, n_z), 'reduce_gradients', (s...  33.9 us
    pallas_call x1, Pallas kernels, shards(): call(functools.partial(gather_kernel, n_col), 'gather_lanes', (shape((2,...  20.9 us
    pallas_call x1, Pallas kernels, shards(): call(functools.partial(combine_kernel, n_col), 'combine_rows', (shape((bl...  10.7 us
    pallas_call x1, Pallas kernels, shards(): call(functools.partial(backward_kernel, key_blocks), 'backward_pairs', (s...  6.03 us
    pallas_call x1, Pallas kernels, shards(): call(functools.partial(forward_kernel, key_blocks), 'forward_pairs', (sha...  4.25 us

profile of v6, /device:TPU:1, one launch (start us, length us, event | category | flops | bytes accessed | tf_op | source)
XLA Modules:
  0.0 79.3 jit_solution(14461273447775049843)
XLA Ops:
  1.3 0.7 convert_bitcast_fusion
  1.9 0.8 fusion.4.own_ref
  2.7 0.0 copy-start
  2.7 0.0 copy-start.1
  2.8 20.9 %gather_lanes.1 = (bf16[2,4,4,64,128]{4,3,2,1,0:T(8,128)(2,1)S(1)}, bf16[2,4,4,64,128]{4,3,2,1,0:T(8,128)(2,1)S(1)}, s32[2,16,128]{2,1,0:T(8,128)S(1)}) custom-call(bf16[144,256]{1,0:T(8,128)(2,1)S(1)} %fusion.4.own_ref), custom_call_target="tpu_custom_call" | custom-call | flops 10000000000 | bytes 10000000 | tf_op jit(solution)/shard_map/gather_lanes/pallas_call | solution.py:582
  23.6 0.0 copy-done
  23.6 0.0 copy-done.1
  23.6 4.3 %forward_pairs.1 = (f32[128,2176]{1,0:T(8,128)S(1)}, f32[2,8,1536]{2,1,0:T(8,128)S(1)}, bf16[17,512,128]{2,1,0:T(8,128)(2,1)S(1)}) custom-call(s32[2,16,128]{2,1,0:T(8,128)S(1)} %get-tuple-element.23.info, bf16[2048,128]{1,0:T(8,128)(2,1)S(1)} %bitcast.15, bf16[2048,128]{1,0:T(8,128)(2,1)S(1)} %bitcast.13, bf16[2048,256]{1,0:T(8,128)(2,1)S(1)} %bitcast.8, ...), custom_call_target="tpu_custom_call" | custom-call | flops 10000000000 | bytes 10000000 | tf_op jit(solution)/shard_map/forward_pairs/pallas_call | solution.py:594
  27.9 10.7 %combine_rows.1 = (f32[16,8,128]{2,1,0:T(8,128)S(1)}, bf16[17,512,128]{2,1,0:T(8,128)(2,1)S(1)}, bf16[128,2048]{1,0:T(8,128)(2,1)S(1)}) custom-call(f32[2,8,1536]{2,1,0:T(8,128)S(1)} %get-tuple-element.27.stat, bf16[2048,128]{1,0:T(8,128)(2,1)S(1)} %bitcast.14, bf16[2048,256]{1,0:T(8,128)(2,1)S(1)} %bitcast.9), custom_call_target="tpu_custom_call" | custom-call | flops 10000000000 | bytes 10000000 | tf_op jit(solution)/shard_map/combine_rows/pallas_call | solution.py:602
  38.7 6.0 %backward_pairs.1 = (f32[128,2176]{1,0:T(8,128)S(1)}, bf16[16,2,128,128]{3,2,1,0:T(8,128)(2,1)S(1)}) custom-call(s32[2,16,128]{2,1,0:T(8,128)S(1)} %get-tuple-element.23.info, bf16[17,512,128]{2,1,0:T(8,128)(2,1)S(1)} %get-tuple-element.26.qbd, bf16[17,512,128]{2,1,0:T(8,128)(2,1)S(1)} %get-tuple-element.28.gbd, bf16[2048,256]{1,0:T(8,128)(2,1)S(1)} %bitcast.10, ...), custom_call_target="tpu_custom_call" | custom-call | flops 10000000000 | bytes 10000000 | tf_op jit(solution)/shard_map/backward_pairs/pallas_call | solution.py:615
  44.7 33.9 %reduce_gradients.1 = (bf16[64,256]{1,0:T(8,128)(2,1)S(1)}, bf16[64,256]{1,0:T(8,128)(2,1)S(1)}, bf16[64,256]{1,0:T(8,128)(2,1)S(1)}, bf16[64,256]{1,0:T(8,128)(2,1)S(1)}) custom-call(f32[128,2176]{1,0:T(8,128)S(1)} %get-tuple-element.31.dq_acc, bf16[16,2,128,128]{3,2,1,0:T(8,128)(2,1)S(1)} %get-tuple-element.32.dkv, ...), custom_call_target="tpu_custom_call" | custom-call | flops 10000000000 | bytes 10000000 | tf_op jit(solution)/shard_map/reduce_gradients/pallas_call | solution.py:626
  78.7 0.7 leave.1
Async XLA Ops:
  2.7 20.9 %copy-start = (bf16[1,2048,256]{2,1,0:T(8,128)(2,1)S(1)}, bf16[1,2048,256]{2,1,0:T(8,128)(2,1)}, u32[]{:S(2)}) copy-start(bf16[1,2048,256]{2,1,0:T(8,128)(2,1)} %param.7) | copy-start | bytes 3145732
  2.7 20.9 %copy-start.1 = (bf16[1,2048,256]{2,1,0:T(8,128)(2,1)S(1)}, bf16[1,2048,256]{2,1,0:T(8,128)(2,1)}, u32[]{:S(2)}) copy-start(bf16[1,2048,256]{2,1,0:T(8,128)(2,1)} %param.8) | copy-start | bytes 3145732
